TPU v7x, 512 devices: a whole 4x8x8 slice. The times are simulated.
512 devices in a mesh: dp: 64 (over x, z, core), head: 8 (over y).
Axes of the slice: x: 4, y: 8, z: 8, core: 2. Of those that a mesh axis runs over, the one named last changes fastest.
Arguments:
- prompt_query: bfloat16 [4096, 8192], P('dp', 'head'), may hold values from -6 to 6
- prompt_key: bfloat16 [4096, 1024], P('dp', 'head'), may hold values from -6 to 6
- prompt_value: bfloat16 [4096, 1024], P('dp', 'head'), may hold values from -6 to 6
- prompt_out: bfloat16 [4096, 8192], P('dp', 'head'), may hold values from -6 to 6
- prompt_grad: bfloat16 [4096, 8192], P('dp', 'head'), may hold values from -40 to 40
- response_query: bfloat16 [64, 64, 8192], P('dp', None, 'head'), may hold values from -6 to 6
- response_key: bfloat16 [64, 64, 1024], P('dp', None, 'head'), may hold values from -6 to 6
- response_value: bfloat16 [64, 64, 1024], P('dp', None, 'head'), may hold values from -6 to 6
- response_out: bfloat16 [64, 64, 8192], P('dp', None, 'head'), may hold values from -6 to 6
- response_grad: bfloat16 [64, 64, 8192], P('dp', None, 'head'), may hold values from -40 to 40
- lengths: int32 [64], P('dp'), may hold values from 1 to 64, 2560 in all
- query_gain: float32 [128], replicated, may hold values from 0.6 to 6
- key_gain: float32 [128], replicated, may hold values from 0.6 to 6
Outputs:
- prompt_dquery: bfloat16 [4096, 8192], P('dp', 'head')
- prompt_dkey: bfloat16 [4096, 1024], P('dp', 'head')
- prompt_dvalue: bfloat16 [4096, 1024], P('dp', 'head')
- response_dquery: bfloat16 [64, 64, 8192], P('dp', None, 'head')
- response_dkey: bfloat16 [64, 64, 1024], P('dp', None, 'head')
- response_dvalue: bfloat16 [64, 64, 1024], P('dp', None, 'head')
- query_dgain: float32 [128], replicated
- key_dgain: float32 [128], replicated
Inputs may be any that keep to these rules, and one draw needn't show every extreme that they name: `lengths`: some response has all 64 tokens live.
All inputs are finite; a program needn't handle non-finite values. No bound on the sum of `lengths` on one device may be relied on, other than what follows from the above.
Results may differ from a plain program's by a relative error of at most 0.012.
The roundings to bfloat16 on the way count: a program that leaves them out, or rounds other values in their place, can miss the bound.
Values may be sent and summed in bfloat16 or wider, within the bound.
No kernel may reach another device: no remote copies, remote signals or barrier semaphores. Data moves between devices by JAX's collectives and lax.ppermute only.
A program may use at most 64 MiB of HBM per device.

v0:
```python
import functools
import math

import jax
import jax.numpy as jnp
from jax import lax
from jax.experimental import pallas as pl
from jax.experimental.pallas import tpu as pltpu
from jax.sharding import Mesh
from jax.sharding import PartitionSpec as P

NX, NZ, NC = 4, 8, 2
HD = 128
GROUPS = 8
ROWS = 64
PCOLS = GROUPS * ROWS
COLS = 2 * PCOLS
BLOCKS = NX * NZ * NC
KEYS = BLOCKS * ROWS
HALF = KEYS // 2
CHUNK = NZ * ROWS
CG = 256
EXTRA = 8
TAIL = 16
INTERPRET = False
epsilon = 1e-06
masked_value = -1e30
SCALING = 1.0 / math.sqrt(HD)
EXP_SCALE = SCALING * math.log2(math.e)


def unit_rows(values):
    inverse = lax.rsqrt(jnp.mean(values * values, axis=-1, keepdims=True) + epsilon)
    return values * inverse, inverse


def norm_back(unit, inverse, grads, gain):
    scaled = grads * gain
    return inverse * (scaled - unit * jnp.mean(unit * scaled, axis=-1, keepdims=True))


def mm(left, right):
    return jnp.dot(left, right, preferred_element_type=jnp.float32)


def two_heads(ref, pair):
    first = ref[:, 2 * pair * HD : (2 * pair + 1) * HD]
    second = ref[:, (2 * pair + 1) * HD : (2 * pair + 2) * HD]
    return jnp.concatenate([first.astype(jnp.float32), second.astype(jnp.float32)], axis=0)


def prepare_kernel(pq_in, pg_in, po_in, rq_in, rg_in, ro_in, qgain, qn, qn_t, gr, gr_t, delta, held, sems):
    f32, bf16 = jnp.float32, jnp.bfloat16
    copies = [
        pltpu.make_async_copy(ref, held.at[i], sems.at[i])
        for i, ref in enumerate((pq_in, rq_in, pg_in, rg_in, po_in, ro_in))
    ]
    for copy in copies:
        copy.start()
    for copy in copies:
        copy.wait()
    gain_q = qgain[...]
    for part in range(2):
        q, g, o = held.at[part], held.at[2 + part], held.at[4 + part]
        for pair in range(GROUPS // 2):
            r0 = part * PCOLS + pair * 2 * ROWS
            rows = slice(r0, r0 + 2 * ROWS)
            unit, _ = unit_rows(two_heads(q, pair))
            normed = (unit * gain_q).astype(bf16)
            qn[rows, :] = normed
            qn_t[:, rows] = normed.astype(f32).T.astype(bf16)
            grads = two_heads(g, pair)
            gr[rows, :] = grads.astype(bf16)
            gr_t[:, rows] = grads.T.astype(bf16)
            product = grads * two_heads(o, pair)
            delta[:, rows] = jnp.sum(product.T, axis=0, keepdims=True)


def prepare(arrays, qgain):
    f32, bf16 = jnp.float32, jnp.bfloat16
    vmem = pl.BlockSpec(memory_space=pltpu.VMEM)
    out_shape = (
        jax.ShapeDtypeStruct((COLS, HD), bf16),
        jax.ShapeDtypeStruct((HD, COLS), bf16),
        jax.ShapeDtypeStruct((COLS, HD), bf16),
        jax.ShapeDtypeStruct((HD, COLS), bf16),
        jax.ShapeDtypeStruct((1, COLS), f32),
    )
    return pl.pallas_call(
        prepare_kernel,
        out_shape=out_shape,
        in_specs=[pl.BlockSpec(memory_space=pl.ANY)] * len(arrays) + [vmem],
        out_specs=tuple([vmem] * len(out_shape)),
        scratch_shapes=[
            pltpu.VMEM((len(arrays), ROWS, GROUPS * HD), bf16),
            pltpu.SemaphoreType.DMA((len(arrays),)),
        ],
        compiler_params=pltpu.CompilerParams(vmem_limit_bytes=8 * 1024 * 1024),
        cost_estimate=pl.CostEstimate(flops=COLS * HD * 40, bytes_accessed=2 << 20, transcendentals=0),
        interpret=INTERPRET,
    )(*arrays, qgain)


def attention_kernel(
    info, pq_in, rq_in, rk_in, rv_in, qn, qn_t, gr, gr_t, delta, kv_own, kv_other, qgain, kgain,
    keep, send, terms, pdq, rdq, rdk, rdv,
    kn, kn_t, vals, kunit, rkn, rkn_t, probs, rprobs, maxima, top, total, factor, dq_t, held, rk, rv,
    sems,
):
    f32, bf16 = jnp.float32, jnp.bfloat16
    kv_refs = (kv_own, kv_other)
    gain_q, gain_k = qgain[...], kgain[...]
    copies = [
        pltpu.make_async_copy(rk_in, rk, sems.at[0]),
        pltpu.make_async_copy(rv_in, rv, sems.at[1]),
        pltpu.make_async_copy(pq_in, held.at[0], sems.at[2]),
        pltpu.make_async_copy(rq_in, held.at[1], sems.at[3]),
    ]
    for copy in copies:
        copy.start()

    k0 = 0
    for ref in kv_refs:
        for at in range(0, ref.shape[0], CHUNK):
            rows = slice(k0, k0 + CHUNK)
            unit, _ = unit_rows(ref[at : at + CHUNK, :HD].astype(f32))
            normed = (unit * gain_k).astype(bf16)
            kunit[rows, :] = unit
            kn[rows, :] = normed
            kn_t[k0 // CHUNK] = normed.astype(f32).T.astype(bf16)
            vals[rows, :] = ref[at : at + CHUNK, HD:]
            k0 += CHUNK

    copies[0].wait()
    copies[1].wait()
    runit, rinv = unit_rows(rk[...].astype(f32))
    rnormed = (runit * gain_k).astype(bf16)
    rkn[...] = rnormed
    rkn_t[...] = rnormed.astype(f32).T.astype(bf16)

    scores = mm(rkn[...], qn_t[:, PCOLS:]) * EXP_SCALE
    key_at = lax.broadcasted_iota(jnp.int32, (ROWS, PCOLS), 0)
    query_at = lax.broadcasted_iota(jnp.int32, (ROWS, PCOLS), 1) & (ROWS - 1)
    scores = jnp.where(key_at <= query_at, scores, masked_value)
    first = jnp.max(scores, axis=0, keepdims=True)
    raised = jnp.exp2(scores - first)
    rprobs[...] = raised
    rfirst = first
    top[:, :PCOLS] = jnp.full((1, PCOLS), masked_value, f32)
    total[:, :PCOLS] = jnp.zeros((1, PCOLS), f32)
    top[:, PCOLS:] = first
    total[:, PCOLS:] = jnp.sum(raised, axis=0, keepdims=True)

    my_x, my_z, my_core = info[1], info[2], info[3]

    def first_pass(j, _):
        at = pl.multiple_of(j * CHUNK, CHUNK)
        key_x = lax.rem(j, NX)
        key_core = jnp.where(j < NX, my_core, 1 - my_core)

        def tile(c0, masked):
            cols = slice(c0, c0 + CG)
            scores = mm(kn[pl.ds(at, CHUNK), :], qn_t[:, cols]) * EXP_SCALE
            if masked:
                row = lax.broadcasted_iota(jnp.int32, (CHUNK, 1), 0)
                key_block = (key_x * NZ + row // ROWS) * NC + key_core
                key_pos = key_block * ROWS + (row & (ROWS - 1))
                query_pos = lax.broadcasted_iota(jnp.int32, (1, CG), 1) & (ROWS - 1)
                query_pos = query_pos + ((my_x * NZ + my_z) * NC + my_core) * ROWS
                scores = jnp.where(key_pos <= query_pos, scores, masked_value)
            old = top[:, cols]
            new = jnp.maximum(old, jnp.max(scores, axis=0, keepdims=True))
            raised = jnp.exp2(scores - new)
            probs[pl.ds(at, CHUNK), cols] = raised
            total[:, cols] = total[:, cols] * jnp.exp2(old - new) + jnp.sum(
                raised, axis=0, keepdims=True
            )
            top[:, cols] = new
            maxima[j, :, cols] = new

        @pl.when(key_x < my_x)
        def _():
            for c0 in range(0, COLS, CG):
                tile(c0, False)

        @pl.when(key_x >= my_x)
        def _():
            for c0 in range(0, COLS, CG):
                tile(c0, c0 < PCOLS)

        return 0

    lax.fori_loop(0, KEYS // CHUNK, first_pass, 0)

    column = lax.broadcasted_iota(jnp.int32, (1, COLS), 1)
    living = (column < PCOLS) | ((column & (ROWS - 1)) < info[0])
    factor[...] = jnp.where(living, 1.0 / total[...], 0.0)
    dq_t[...] = jnp.zeros_like(dq_t)

    def second_pass(out, base, j, carry):
        key_terms, largest_k, largest_v = carry
        at = pl.multiple_of(j * CHUNK, CHUNK)
        here = pl.multiple_of((j - base) * CHUNK, CHUNK)
        values = vals[pl.ds(at, CHUNK), :]
        keys_t = kn_t[j]
        dkey = jnp.zeros((CHUNK, HD), f32)
        dvalue = jnp.zeros((CHUNK, HD), f32)
        for c0 in range(0, COLS, CG):
            cols = slice(c0, c0 + CG)
            scale = jnp.exp2(maxima[j, :, cols] - top[:, cols]) * factor[:, cols]
            weights = probs[pl.ds(at, CHUNK), cols] * scale
            dweights = mm(values, gr_t[:, cols])
            dscores = (weights * (dweights - delta[:, cols])).astype(bf16)
            dvalue = dvalue + mm(weights.astype(bf16), gr[cols, :])
            dkey = dkey + mm(dscores, qn[cols, :])
            dq_t[:, cols] = dq_t[:, cols] + mm(keys_t, dscores)
        dkey = dkey * SCALING
        out[pl.ds(here, CHUNK), :HD] = dkey
        out[pl.ds(here, CHUNK), HD:] = dvalue
        products = dkey * kunit[pl.ds(at, CHUNK), :]
        eights = (CHUNK // 8, 8, HD)
        return (
            key_terms + jnp.sum(products.reshape(eights), axis=0),
            jnp.maximum(largest_k, jnp.max(jnp.abs(dkey).reshape(eights), axis=0)),
            jnp.maximum(largest_v, jnp.max(jnp.abs(dvalue).reshape(eights), axis=0)),
        )

    half = HALF // CHUNK
    zero = jnp.zeros((8, HD), f32)
    key_terms = zero
    for out, base in ((send, half), (keep, 0)):
        key_terms, largest_k, largest_v = lax.fori_loop(
            base, base + half, functools.partial(second_pass, out, base), (key_terms, zero, zero)
        )
        out[HALF:, :HD] = jnp.broadcast_to(jnp.max(largest_k, axis=0, keepdims=True), (EXTRA, HD))
        out[HALF:, HD:] = jnp.broadcast_to(jnp.max(largest_v, axis=0, keepdims=True), (EXTRA, HD))

    right = slice(PCOLS, COLS)
    scale = jnp.exp2(rfirst - top[:, right]) * factor[:, right]
    weights = rprobs[...] * scale
    dweights = mm(rv[...], gr_t[:, right])
    dscores = (weights * (dweights - delta[:, right])).astype(bf16)
    rdv[...] = mm(weights.astype(bf16), gr[right, :]).astype(bf16)
    dkey = mm(dscores, qn[right, :]) * SCALING
    rdk[...] = norm_back(runit, rinv, dkey, gain_k).astype(bf16)
    dq_t[:, right] = dq_t[:, right] + mm(rkn_t[...], dscores)
    key_terms = jnp.sum(key_terms, axis=0, keepdims=True)
    key_terms = key_terms + jnp.sum(dkey * runit, axis=0, keepdims=True)

    query_terms = jnp.zeros((1, HD), f32)
    copies[2].wait()
    copies[3].wait()
    for part, out in enumerate((pdq, rdq)):
        q = held.at[part]
        for pair in range(GROUPS // 2):
            r0 = part * PCOLS + pair * 2 * ROWS
            unit, inverse = unit_rows(two_heads(q, pair))
            dquery = dq_t[:, r0 : r0 + 2 * ROWS].T * SCALING
            query_terms = query_terms + jnp.sum(dquery * unit, axis=0, keepdims=True)
            raw = norm_back(unit, inverse, dquery, gain_q).astype(bf16)
            out[:, 2 * pair * HD : (2 * pair + 1) * HD] = raw[:ROWS]
            out[:, (2 * pair + 1) * HD : (2 * pair + 2) * HD] = raw[ROWS:]

    terms[:, :HD] = jnp.broadcast_to(query_terms, (EXTRA, HD))
    terms[:, HD:] = jnp.broadcast_to(key_terms, (EXTRA, HD))


def attention(info, raw, arrays):
    f32, bf16 = jnp.float32, jnp.bfloat16
    vmem = pl.BlockSpec(memory_space=pltpu.VMEM)
    smem = pl.BlockSpec(memory_space=pltpu.SMEM)
    anywhere = pl.BlockSpec(memory_space=pl.ANY)
    out_shape = (
        jax.ShapeDtypeStruct((HALF + EXTRA, 2 * HD), f32),
        jax.ShapeDtypeStruct((HALF + EXTRA, 2 * HD), f32),
        jax.ShapeDtypeStruct((EXTRA, 2 * HD), f32),
        jax.ShapeDtypeStruct((ROWS, GROUPS * HD), bf16),
        jax.ShapeDtypeStruct((ROWS, GROUPS * HD), bf16),
        jax.ShapeDtypeStruct((ROWS, HD), bf16),
        jax.ShapeDtypeStruct((ROWS, HD), bf16),
    )
    chunks = KEYS // CHUNK
    scratch = [
        pltpu.VMEM((KEYS, HD), bf16),
        pltpu.VMEM((chunks, HD, CHUNK), bf16),
        pltpu.VMEM((KEYS, HD), bf16),
        pltpu.VMEM((KEYS, HD), f32),
        pltpu.VMEM((ROWS, HD), bf16),
        pltpu.VMEM((HD, ROWS), bf16),
        pltpu.VMEM((KEYS, COLS), f32),
        pltpu.VMEM((ROWS, PCOLS), f32),
        pltpu.VMEM((chunks, 1, COLS), f32),
        pltpu.VMEM((1, COLS), f32),
        pltpu.VMEM((1, COLS), f32),
        pltpu.VMEM((1, COLS), f32),
        pltpu.VMEM((HD, COLS), f32),
        pltpu.VMEM((2, ROWS, GROUPS * HD), bf16),
        pltpu.VMEM((ROWS, HD), bf16),
        pltpu.VMEM((ROWS, HD), bf16),
        pltpu.SemaphoreType.DMA((4,)),
    ]
    return pl.pallas_call(
        attention_kernel,
        out_shape=out_shape,
        in_specs=[smem] + [anywhere] * len(raw) + [vmem] * len(arrays),
        out_specs=tuple([vmem] * len(out_shape)),
        scratch_shapes=scratch,
        compiler_params=pltpu.CompilerParams(vmem_limit_bytes=48 * 1024 * 1024),
        cost_estimate=pl.CostEstimate(
            flops=10 * KEYS * COLS * HD, bytes_accessed=8 << 20, transcendentals=KEYS * COLS
        ),
        interpret=INTERPRET,
    )(info, *raw, *arrays)


def exchange(array, axis):
    return lax.all_to_all(array, axis, 0, 0, tiled=True)


def exchange_halves(message, axis):
    halves = message.astype(jnp.float16).reshape(-1, 2 * HD)
    return exchange(halves, axis).astype(jnp.float32).reshape(message.shape)


def swap_core(array):
    return lax.ppermute(array, "core", [(0, 1), (1, 0)])


def pack_message(message, rows, count, blocks, largest, terms):
    exponent = jnp.clip(jnp.floor(jnp.log2(jnp.maximum(largest, 1e-37))), -100.0, 100.0)
    scale = jnp.exp2(14.0 - exponent)
    term_exponent = jnp.clip(
        jnp.floor(jnp.log2(jnp.maximum(jnp.abs(terms), 1e-37))), -100.0, 100.0
    )
    scaled = terms * jnp.exp2(14.0 - term_exponent)
    high = scaled.astype(jnp.bfloat16).astype(jnp.float32)
    low = (scaled - high) * 256.0
    row = lax.broadcasted_iota(jnp.int32, (TAIL, 2 * HD), 0)
    tail = jnp.where(row == 2, exponent, term_exponent)
    tail = jnp.where(row == 0, high, jnp.where(row == 1, low, tail))
    for i in range(count):
        message[i, :rows] = blocks(i) * scale
        message[i, rows:] = tail


def unpack_message(message, rows, count):
    total = jnp.zeros((rows, 2 * HD), jnp.float32)
    terms = jnp.zeros((1, 2 * HD), jnp.float32)
    for i in range(count):
        tail = message[i, rows:]
        total = total + message[i, :rows] * jnp.exp2(tail[2:3] - 14.0)
        terms = terms + (tail[0:1] + tail[1:2] * (1.0 / 256.0)) * jnp.exp2(tail[3:4] - 14.0)
    return total, terms


def first_stage_kernel(keep, got, terms, message):
    rows = NZ * ROWS
    largest = keep[HALF : HALF + 1, :] + got[HALF : HALF + 1, :]

    def blocks(i):
        return keep[i * rows : (i + 1) * rows, :] + got[i * rows : (i + 1) * rows, :]

    pack_message(message, rows, NX, blocks, largest, terms[0:1, :])


def second_stage_kernel(got, message):
    total, terms = unpack_message(got, NZ * ROWS, NX)
    largest = jnp.max(jnp.abs(total), axis=0, keepdims=True)
    pack_message(message, ROWS, NZ, lambda i: total[i * ROWS : (i + 1) * ROWS], largest, terms)


def last_stage_kernel(got, keys, kgain, pdk, pdv, query_terms, key_terms):
    total, terms = unpack_message(got, ROWS, NZ)
    unit, inverse = unit_rows(keys[...].astype(jnp.float32))
    pdk[...] = norm_back(unit, inverse, total[:, :HD], kgain[...]).astype(jnp.bfloat16)
    pdv[...] = total[:, HD:].astype(jnp.bfloat16)
    query_terms[...] = terms[:, :HD]
    key_terms[...] = terms[:, HD:]


def small_kernel(body, out_shape, *arrays):
    vmem = pl.BlockSpec(memory_space=pltpu.VMEM)
    outs = vmem if isinstance(out_shape, jax.ShapeDtypeStruct) else tuple([vmem] * len(out_shape))
    return pl.pallas_call(
        body,
        out_shape=out_shape,
        in_specs=[vmem] * len(arrays),
        out_specs=outs,
        compiler_params=pltpu.CompilerParams(vmem_limit_bytes=16 * 1024 * 1024),
        cost_estimate=pl.CostEstimate(flops=1 << 20, bytes_accessed=4 << 20, transcendentals=0),
        interpret=INTERPRET,
    )(*arrays)


def sum_over_heads(terms):
    heads = lax.axis_size("head")
    step = 1
    while step < heads:
        pairs = [(i, i ^ step) for i in range(heads)]
        terms = terms + lax.ppermute(terms, "head", pairs)
        step *= 2
    return terms + swap_core(terms)


def per_device(
    prompt_query,
    prompt_key,
    prompt_value,
    prompt_out,
    prompt_grad,
    response_query,
    response_key,
    response_value,
    response_out,
    response_grad,
    lengths,
    query_gain,
    key_gain,
):
    line = NX * NZ
    place = [lax.axis_index(name).astype(jnp.int32)[None] for name in ("x", "z", "core")]
    info = jnp.concatenate([lengths, *place])
    qgain, kgain = query_gain.reshape(1, HD), key_gain.reshape(1, HD)

    local = jnp.concatenate([prompt_key, prompt_value], axis=1)
    copies = jnp.broadcast_to(local[None], (line,) + local.shape)
    own = exchange(copies.reshape(line * ROWS, 2 * HD), ("x", "z"))
    raw = [prompt_query, prompt_grad, prompt_out, response_query[0], response_grad[0], response_out[0]]
    prepared = prepare(raw, qgain)
    own, prepared = lax.optimization_barrier((own, prepared))
    other = swap_core(own)
    keep, give, terms, pdq, rdq, rdk, rdv = attention(
        info,
        [prompt_query, response_query[0], response_key[0], response_value[0]],
        [*prepared, own, other, qgain, kgain],
    )

    got = swap_core(give)
    terms = sum_over_heads(terms)
    rows = NZ * ROWS + TAIL
    message = small_kernel(
        first_stage_kernel, jax.ShapeDtypeStruct((NX, rows, 2 * HD), jnp.float32), keep, got, terms
    )
    message = exchange_halves(message, "x")
    rows = ROWS + TAIL
    message = small_kernel(
        second_stage_kernel, jax.ShapeDtypeStruct((NZ, rows, 2 * HD), jnp.float32), message
    )
    message = exchange_halves(message, "z")
    block = jax.ShapeDtypeStruct((ROWS, HD), jnp.bfloat16)
    gain = jax.ShapeDtypeStruct((1, HD), jnp.float32)
    pdk, pdv, query_total, key_total = small_kernel(
        last_stage_kernel, (block, block, gain, gain), message, prompt_key, kgain
    )
    return pdq, pdk, pdv, rdq[None], rdk[None], rdv[None], query_total[0], key_total[0]


def solution(mesh):
    heads = mesh.devices.shape[1]
    mesh = Mesh(mesh.devices.reshape(NX, NZ, NC, heads), ("x", "z", "core", "head"))
    dp = ("x", "z", "core")
    columns, stacked = P(dp, "head"), P(dp, None, "head")
    in_specs = (columns,) * 5 + (stacked,) * 5 + (P(dp), P(), P())
    out_specs = (columns,) * 3 + (stacked,) * 3 + (P(), P())
    return jax.shard_map(
        per_device, mesh=mesh, in_specs=in_specs, out_specs=out_specs, check_vma=False
    )
```

profile of v0, /device:TPU:1, one launch (start us, length us, event | category | flops | bytes accessed | tf_op | source)
XLA Modules:
  0.0 134.3 jit_solution(4298555745874228366)
XLA Ops:
  0.6 0.0 copy-start.4
  0.6 0.0 copy-start.8
  0.7 0.0 copy-start.2
  0.7 0.0 copy-start.3
  0.7 0.0 copy-start.5
  0.7 0.0 copy-start
  0.7 0.0 copy-start.1
  0.7 0.0 copy-start.7
  0.7 0.0 copy-start.14
  0.7 0.0 copy-start.13
  0.7 0.9 pad_maximum_fusion
  1.6 1.1 broadcast_in_dim.27
  2.7 13.7 %all-to-all-start = ((bf16[32,64,256]{2,1,0:T(8,128)(2,1)}), bf16[32,64,256]{2,1,0:T(8,128)(2,1)S(1)}, u32[]{:S(2)}, u32[]{:S(2)}) async-start(bf16[32,64,256]{2,1,0:T(8,128)(2,1)} %broadcast_in_dim.27), calls=%async_computation | async-start | bytes 2097152 | tf_op jit(solution)/shard_map/all_to_all | solution.py:317
  16.5 0.0 copy-done.4
  16.5 0.0 copy-done.8
  16.5 0.0 copy-done.2
  16.5 0.0 copy-done.3
  16.5 0.0 copy-done.5
  16.5 0.0 copy-done
  16.5 0.0 copy-done.1
  16.5 1.7 %shard_map.188 = (bf16[1024,128]{1,0:T(8,128)(2,1)S(1)}, bf16[128,1024]{1,0:T(8,128)(2,1)S(1)}, bf16[1024,128]{1,0:T(8,128)(2,1)S(1)}, bf16[128,1024]{1,0:T(8,128)(2,1)S(1)}, f32[1,1024]{1,0:T(1,128)S(1)}) custom-call(bf16[64,1024]{1,0:T(8,128)(2,1)S(1)} %copy-done.4, bf16[64,1024]{1,0:T(8,128)(2,1)S(1)} %copy-done, bf16[64,1024]{1,0:T(8,128)(2,1)S(1)} %copy-done.1, ...), custom_call_target="tpu_custom_call" | custom-call | flops 5242880 | bytes 2097152 | tf_op jit(solution)/shard_map/pallas_call | solution.py:89
  18.2 0.0 copy-start.9
  18.2 0.7 copy-done.9
  18.9 0.0 copy-start.11
  18.9 0.7 copy-done.11
  19.6 21.5 %all-to-all-done = bf16[32,64,256]{2,1,0:T(8,128)(2,1)S(1)} async-done(((bf16[32,64,256]{2,1,0:T(8,128)(2,1)}), bf16[32,64,256]{2,1,0:T(8,128)(2,1)S(1)}, u32[]{:S(2)}, u32[]{:S(2)}) %all-to-all-start) | async-done | bytes 1048608 | tf_op jit(solution)/shard_map/all_to_all | solution.py:317
  41.1 6.9 %collective-permute-start = (bf16[2048,256]{1,0:T(8,128)(2,1)S(1)}, bf16[2048,256]{1,0:T(8,128)(2,1)S(1)}, u32[]{:S(2)}, u32[]{:S(2)}) collective-permute-start(bf16[2048,256]{1,0:T(8,128)(2,1)S(1)} %bitcast.16), channel_id=1, source_target_pairs={{0,8},{8,0},{1,9},{9,1},{2,10},{10,2},{3,11},{11,3},{4,12},{12,4},... | collective-permute-start | bytes 3145736 | tf_op jit(solution)/shard_map/ppermute | solution.py:326
  48.6 0.1 pad_add_fusion.info
  48.7 1.5 %collective-permute-done.kv_other = bf16[2048,256]{1,0:T(8,128)(2,1)S(1)} collective-permute-done((bf16[2048,256]{1,0:T(8,128)(2,1)S(1)}, bf16[2048,256]{1,0:T(8,128)(2,1)S(1)}, u32[]{:S(2)}, u32[]{:S(2)}) %collective-permute-start) | collective-permute-done | bytes 1048608 | tf_op jit(solution)/shard_map/ppermute | solution.py:326
  50.2 0.0 copy-done.7
  50.2 0.0 copy-done.14
  50.2 0.0 copy-done.13
  50.2 0.0 copy-start.10
  50.2 0.9 copy-done.10
  51.2 0.0 copy-start.12
  51.2 0.9 copy-done.12
  52.1 22.2 %shard_map.189 = (f32[2056,256]{1,0:T(8,128)S(1)}, f32[2056,256]{1,0:T(8,128)}, f32[8,256]{1,0:T(8,128)S(1)}, bf16[64,1024]{1,0:T(8,128)(2,1)}, bf16[64,1024]{1,...) custom-call(s32[4]{0:T(128)S(1)} %pad_add_fusion.info, bf16[64,1024]{1,0:T(8,128)(2,1)S(1)} %copy-done.4, ...), custom_call_target="tpu_custom_call" | custom-call | flops 5368709120 | bytes 8388608 | tf_op jit(solution)/shard_map/pallas_call | solution.py:302
  74.4 2.3 %collective-permute-start.1 = (f32[2056,256]{1,0:T(8,128)}, f32[2056,256]{1,0:T(8,128)S(1)}, u32[]{:S(2)}, u32[]{:S(2)}) collective-permute-start(f32[2056,256]{1,0:T(8,128)} %get-tuple-element.43), channel_id=1, source_target_pairs={{0,8},{8,0},{1,9},{9,1},{2,10},{10,2},{3,11},{11,3},{4,12},{12,4},... | collective-permute-start | bytes 6316040 | tf_op jit(solution)/shard_map/ppermute | solution.py:326
  76.7 3.2 %collective-permute-start.2 = (f32[8,256]{1,0:T(8,128)S(1)}, f32[8,256]{1,0:T(8,128)S(1)}, u32[]{:S(2)}, u32[]{:S(2)}) collective-permute-start(f32[8,256]{1,0:T(8,128)S(1)} %get-tuple-element.44), channel_id=1, source_target_pairs={{0,1},{1,0},{2,3},{3,2},{4,5},{5,4},{6,7},{7,6},{8,9},{9,8},{10,11... | collective-permute-start | bytes 24584 | tf_op jit(solution)/shard_map/ppermute | solution.py:400
  79.9 1.2 collective-permute-done.2
  81.1 4.2 %collective-permute-start.3 = (f32[8,256]{1,0:T(8,128)S(1)}, f32[8,256]{1,0:T(8,128)S(1)}, u32[]{:S(2)}, u32[]{:S(2)}) collective-permute-start(f32[8,256]{1,0:T(8,128)S(1)} %add.12), channel_id=1, source_target_pairs={{0,2},{1,3},{2,0},{3,1},{4,6},{5,7},{6,4},{7,5},{8,10},{9,11},{10,... | collective-permute-start | bytes 24584 | tf_op jit(solution)/shard_map/ppermute | solution.py:400
  85.3 1.1 collective-permute-done.3
  86.3 7.4 %collective-permute-start.4 = (f32[8,256]{1,0:T(8,128)S(1)}, f32[8,256]{1,0:T(8,128)S(1)}, u32[]{:S(2)}, u32[]{:S(2)}) collective-permute-start(f32[8,256]{1,0:T(8,128)S(1)} %add.13), channel_id=1, source_target_pairs={{0,4},{1,5},{2,6},{3,7},{4,0},{5,1},{6,2},{7,3},{8,12},{9,13},{10,... | collective-permute-start | bytes 24584 | tf_op jit(solution)/shard_map/ppermute | solution.py:400
  93.8 1.0 collective-permute-done.4
  94.8 5.3 %collective-permute-start.5 = (f32[8,256]{1,0:T(8,128)S(1)}, f32[8,256]{1,0:T(8,128)S(1)}, u32[]{:S(2)}, u32[]{:S(2)}) collective-permute-start(f32[8,256]{1,0:T(8,128)S(1)} %add.14), channel_id=1, source_target_pairs={{0,8},{8,0},{1,9},{9,1},{2,10},{10,2},{3,11},{11,3},{4,12},{12,4},... | collective-permute-start | bytes 24584 | tf_op jit(solution)/shard_map/ppermute | solution.py:326
  100.1 0.8 collective-permute-done.5
  101.0 0.0 collective-permute-done.1.got
  101.0 0.2 shard_map.190
  101.2 0.2 convert_element_type.14
  101.4 17.4 %all_to_all.21 = f16[4,528,256]{2,1,0:T(8,128)(2,1)S(1)} all-to-all(f16[4,528,256]{2,1,0:T(8,128)(2,1)S(1)} %convert_element_type.14), channel_id=1, replica_groups=mesh['x'=4,'z'=8,'core'=2,'head'=8] {'x'}, dimensions={0} | all-to-all | bytes 2162688 | tf_op jit(solution)/shard_map/all_to_all | solution.py:317
  118.8 0.2 convert_element_type.15.got
  119.0 0.0 copy-start.6
  119.0 0.2 shard_map.191
  119.2 0.1 convert_element_type.16
  119.3 14.1 %all_to_all.22 = f16[8,80,256]{2,1,0:T(8,128)(2,1)S(1)} all-to-all(f16[8,80,256]{2,1,0:T(8,128)(2,1)S(1)} %convert_element_type.16), channel_id=1, replica_groups=mesh['x'=4,'z'=8,'core'=2,'head'=8] {'z'}, dimensions={0} | all-to-all | bytes 655360 | tf_op jit(solution)/shard_map/all_to_all | solution.py:317
  133.4 0.1 convert_element_type.17.got
  133.5 0.0 copy-done.6
  133.5 0.8 shard_map.192
  (4 shorter events, 0.0 us)
Async XLA Ops:
  0.6 15.8 %copy-start.4 = (bf16[64,1024]{1,0:T(8,128)(2,1)S(1)}, bf16[64,1024]{1,0:T(8,128)(2,1)}, u32[]{:S(2)}) copy-start(bf16[64,1024]{1,0:T(8,128)(2,1)} %pq_in.3) | copy-start | bytes 393220
  0.6 15.8 %copy-start.8 = (f32[128]{0:T(128)S(1)}, f32[128]{0:T(128)}, u32[]{:S(2)}) copy-start(f32[128]{0:T(128)} %param.24) | copy-start | bytes 1540
  0.7 15.8 %copy-start.2 = (bf16[1,64,1024]{2,1,0:T(8,128)(2,1)S(1)}, bf16[1,64,1024]{2,1,0:T(8,128)(2,1)}, u32[]{:S(2)}) copy-start(bf16[1,64,1024]{2,1,0:T(8,128)(2,1)} %param.22) | copy-start | bytes 393220
  0.7 15.8 %copy-start.3 = (bf16[1,64,1024]{2,1,0:T(8,128)(2,1)S(1)}, bf16[1,64,1024]{2,1,0:T(8,128)(2,1)}, u32[]{:S(2)}) copy-start(bf16[1,64,1024]{2,1,0:T(8,128)(2,1)} %param.21) | copy-start | bytes 393220
  0.7 15.8 %copy-start.5 = (bf16[1,64,1024]{2,1,0:T(8,128)(2,1)S(1)}, bf16[1,64,1024]{2,1,0:T(8,128)(2,1)}, u32[]{:S(2)}) copy-start(bf16[1,64,1024]{2,1,0:T(8,128)(2,1)} %param.18) | copy-start | bytes 393220
  0.7 15.8 %copy-start = (bf16[64,1024]{1,0:T(8,128)(2,1)S(1)}, bf16[64,1024]{1,0:T(8,128)(2,1)}, u32[]{:S(2)}) copy-start(bf16[64,1024]{1,0:T(8,128)(2,1)} %pg_in.1) | copy-start | bytes 393220
  0.7 15.8 %copy-start.1 = (bf16[64,1024]{1,0:T(8,128)(2,1)S(1)}, bf16[64,1024]{1,0:T(8,128)(2,1)}, u32[]{:S(2)}) copy-start(bf16[64,1024]{1,0:T(8,128)(2,1)} %po_in.1) | copy-start | bytes 393220
  0.7 49.5 %copy-start.7 = (f32[128]{0:T(128)S(1)}, f32[128]{0:T(128)}, u32[]{:S(2)}) copy-start(f32[128]{0:T(128)} %param.25) | copy-start | bytes 1540
  0.7 49.5 %copy-start.14 = (bf16[1,64,128]{2,1,0:T(8,128)(2,1)S(1)}, bf16[1,64,128]{2,1,0:T(8,128)(2,1)}, u32[]{:S(2)}) copy-start(bf16[1,64,128]{2,1,0:T(8,128)(2,1)} %param.20) | copy-start | bytes 49156
  0.7 49.5 %copy-start.13 = (bf16[1,64,128]{2,1,0:T(8,128)(2,1)S(1)}, bf16[1,64,128]{2,1,0:T(8,128)(2,1)}, u32[]{:S(2)}) copy-start(bf16[1,64,128]{2,1,0:T(8,128)(2,1)} %param.19) | copy-start | bytes 49156
  2.7 38.3 %all-to-all-start = ((bf16[32,64,256]{2,1,0:T(8,128)(2,1)}), bf16[32,64,256]{2,1,0:T(8,128)(2,1)S(1)}, u32[]{:S(2)}, u32[]{:S(2)}) async-start(bf16[32,64,256]{2,1,0:T(8,128)(2,1)} %broadcast_in_dim.27), calls=%async_computation | async-start | bytes 2097152 | tf_op jit(solution)/shard_map/all_to_all | solution.py:317
  18.2 0.7 copy-start.9
  18.9 0.7 copy-start.11
  41.1 9.1 %collective-permute-start = (bf16[2048,256]{1,0:T(8,128)(2,1)S(1)}, bf16[2048,256]{1,0:T(8,128)(2,1)S(1)}, u32[]{:S(2)}, u32[]{:S(2)}) collective-permute-start(bf16[2048,256]{1,0:T(8,128)(2,1)S(1)} %bitcast.16), channel_id=1, source_target_pairs={{0,8},{8,0},{1,9},{9,1},{2,10},{10,2},{3,11},{11,3},{4,12},{12,4},... | collective-permute-start | bytes 3145736 | tf_op jit(solution)/shard_map/ppermute | solution.py:326
  50.2 1.0 copy-start.10
  51.2 0.9 copy-start.12
  74.4 26.6 %collective-permute-start.1 = (f32[2056,256]{1,0:T(8,128)}, f32[2056,256]{1,0:T(8,128)S(1)}, u32[]{:S(2)}, u32[]{:S(2)}) collective-permute-start(f32[2056,256]{1,0:T(8,128)} %get-tuple-element.43), channel_id=1, source_target_pairs={{0,8},{8,0},{1,9},{9,1},{2,10},{10,2},{3,11},{11,3},{4,12},{12,4},... | collective-permute-start | bytes 6316040 | tf_op jit(solution)/shard_map/ppermute | solution.py:326
  76.7 4.4 %collective-permute-start.2 = (f32[8,256]{1,0:T(8,128)S(1)}, f32[8,256]{1,0:T(8,128)S(1)}, u32[]{:S(2)}, u32[]{:S(2)}) collective-permute-start(f32[8,256]{1,0:T(8,128)S(1)} %get-tuple-element.44), channel_id=1, source_target_pairs={{0,1},{1,0},{2,3},{3,2},{4,5},{5,4},{6,7},{7,6},{8,9},{9,8},{10,11... | collective-permute-start | bytes 24584 | tf_op jit(solution)/shard_map/ppermute | solution.py:400
  81.1 5.3 %collective-permute-start.3 = (f32[8,256]{1,0:T(8,128)S(1)}, f32[8,256]{1,0:T(8,128)S(1)}, u32[]{:S(2)}, u32[]{:S(2)}) collective-permute-start(f32[8,256]{1,0:T(8,128)S(1)} %add.12), channel_id=1, source_target_pairs={{0,2},{1,3},{2,0},{3,1},{4,6},{5,7},{6,4},{7,5},{8,10},{9,11},{10,... | collective-permute-start | bytes 24584 | tf_op jit(solution)/shard_map/ppermute | solution.py:400
  86.3 8.5 %collective-permute-start.4 = (f32[8,256]{1,0:T(8,128)S(1)}, f32[8,256]{1,0:T(8,128)S(1)}, u32[]{:S(2)}, u32[]{:S(2)}) collective-permute-start(f32[8,256]{1,0:T(8,128)S(1)} %add.13), channel_id=1, source_target_pairs={{0,4},{1,5},{2,6},{3,7},{4,0},{5,1},{6,2},{7,3},{8,12},{9,13},{10,... | collective-permute-start | bytes 24584 | tf_op jit(solution)/shard_map/ppermute | solution.py:400
  94.8 6.1 %collective-permute-start.5 = (f32[8,256]{1,0:T(8,128)S(1)}, f32[8,256]{1,0:T(8,128)S(1)}, u32[]{:S(2)}, u32[]{:S(2)}) collective-permute-start(f32[8,256]{1,0:T(8,128)S(1)} %add.14), channel_id=1, source_target_pairs={{0,8},{8,0},{1,9},{9,1},{2,10},{10,2},{3,11},{11,3},{4,12},{12,4},... | collective-permute-start | bytes 24584 | tf_op jit(solution)/shard_map/ppermute | solution.py:326
  119.0 14.5 %copy-start.6 = (bf16[64,128]{1,0:T(8,128)(2,1)S(1)}, bf16[64,128]{1,0:T(8,128)(2,1)}, u32[]{:S(2)}) copy-start(bf16[64,128]{1,0:T(8,128)(2,1)} %keys.1) | copy-start | bytes 49156
where the time goes:
time: 137 us; the launch traced here: 134 us
  starting transfers between devices  43 us (31%)
  blocking collectives  31.6 us (23%)
  waiting for transfers between devices  27.1 us (20%)
  Pallas kernels  25.1 us (18%)
  local copies, waits for them, and re-layouts  4.45 us (3%)
  between operations  1.57 us (1%)
  other arithmetic  1.46 us (1%)
    all_to_all x2, blocking collectives, exchange(): return lax.all_to_all(array, axis, 0, 0, tiled=True)  31.6 us
    pallas_call x1, Pallas kernels, attention(): pl.pallas_call(attention_kernel, out_shape=out_shape, in_specs=[smem] + [...  22.2 us
    all_to_all x1, waiting for transfers between devices, exchange(): return lax.all_to_all(array, axis, 0, 0, tiled=True)  21.5 us
    ppermute x3, starting transfers between devices, sum_over_heads(): terms = terms + lax.ppermute(terms, 'head', pairs)  14.9 us
    ppermute x3, starting transfers between devices, swap_core(): return lax.ppermute(array, 'core', [(0, 1), (1, 0)])  14.5 us
    all_to_all x1, starting transfers between devices, exchange(): return lax.all_to_all(array, axis, 0, 0, tiled=True)  13.7 us
    unnamed x30, local copies, waits for them, and re-layouts  3.32 us
    ppermute x3, waiting for transfers between devices, sum_over_heads(): terms = terms + lax.ppermute(terms, 'head', pairs)  3.27 us
  transfers between devices with their start and end apart: 7, of which 6 were waited for; matrix products, arithmetic and copies ran while one was open for 0% of the time, Pallas kernels for 1%

commit v1 on v0

--- a/solution.py
+++ b/solution.py
@@ -49,12 +49,15 @@
     return jnp.concatenate([first.astype(jnp.float32), second.astype(jnp.float32)], axis=0)
 
 
-def prepare_kernel(pq_in, pg_in, po_in, rq_in, rg_in, ro_in, qgain, qn, qn_t, gr, gr_t, delta, held, sems):
+def prepare_kernel(
+    pq_in, pg_in, po_in, rq_in, rg_in, ro_in, gain_in, qn, qn_t, gr, gr_t, delta, held, qgain, sems
+):
     f32, bf16 = jnp.float32, jnp.bfloat16
     copies = [
         pltpu.make_async_copy(ref, held.at[i], sems.at[i])
         for i, ref in enumerate((pq_in, rq_in, pg_in, rg_in, po_in, ro_in))
     ]
+    copies.append(pltpu.make_async_copy(gain_in, qgain, sems.at[len(copies)]))
     for copy in copies:
         copy.start()
     for copy in copies:
@@ -89,35 +92,48 @@
     return pl.pallas_call(
         prepare_kernel,
         out_shape=out_shape,
-        in_specs=[pl.BlockSpec(memory_space=pl.ANY)] * len(arrays) + [vmem],
+        in_specs=[pl.BlockSpec(memory_space=pl.ANY)] * (len(arrays) + 1),
         out_specs=tuple([vmem] * len(out_shape)),
         scratch_shapes=[
             pltpu.VMEM((len(arrays), ROWS, GROUPS * HD), bf16),
-            pltpu.SemaphoreType.DMA((len(arrays),)),
+            pltpu.VMEM((1, HD), f32),
+            pltpu.SemaphoreType.DMA((len(arrays) + 1,)),
         ],
-        compiler_params=pltpu.CompilerParams(vmem_limit_bytes=8 * 1024 * 1024),
+        compiler_params=pltpu.CompilerParams(vmem_limit_bytes=56 * 1024 * 1024),
         cost_estimate=pl.CostEstimate(flops=COLS * HD * 40, bytes_accessed=2 << 20, transcendentals=0),
         interpret=INTERPRET,
     )(*arrays, qgain)
 
 
 def attention_kernel(
-    info, pq_in, rq_in, rk_in, rv_in, qn, qn_t, gr, gr_t, delta, kv_own, kv_other, qgain, kgain,
-    keep, send, terms, pdq, rdq, rdk, rdv,
+    info, own_in, other_in, kgain_in, rk_in, rv_in, qn_in, qn_t_in, gr_in, gr_t_in, delta_in, qgain_in,
+    pq_in, rq_in, keep, send, terms, pdq, rdq, rdk, rdv,
     kn, kn_t, vals, kunit, rkn, rkn_t, probs, rprobs, maxima, top, total, factor, dq_t, held, rk, rv,
-    sems,
+    weights_b, dscores_b, qn, qn_t, gr, gr_t, delta, qgain, kgain, kv_own, kv_other, sems,
 ):
     f32, bf16 = jnp.float32, jnp.bfloat16
     kv_refs = (kv_own, kv_other)
-    gain_q, gain_k = qgain[...], kgain[...]
-    copies = [
-        pltpu.make_async_copy(rk_in, rk, sems.at[0]),
-        pltpu.make_async_copy(rv_in, rv, sems.at[1]),
-        pltpu.make_async_copy(pq_in, held.at[0], sems.at[2]),
-        pltpu.make_async_copy(rq_in, held.at[1], sems.at[3]),
-    ]
+    moves = (
+        (own_in, kv_own),
+        (other_in, kv_other),
+        (kgain_in, kgain),
+        (rk_in, rk),
+        (rv_in, rv),
+        (qn_in, qn),
+        (qn_t_in, qn_t),
+        (gr_in, gr),
+        (gr_t_in, gr_t),
+        (delta_in, delta),
+        (qgain_in, qgain),
+        (pq_in, held.at[0]),
+        (rq_in, held.at[1]),
+    )
+    copies = [pltpu.make_async_copy(src, dst, sems.at[i]) for i, (src, dst) in enumerate(moves)]
     for copy in copies:
         copy.start()
+    for copy in copies[:3]:
+        copy.wait()
+    gain_k = kgain[...]
 
     k0 = 0
     for ref in kv_refs:
@@ -131,8 +147,9 @@
             vals[rows, :] = ref[at : at + CHUNK, HD:]
             k0 += CHUNK
 
-    copies[0].wait()
-    copies[1].wait()
+    for copy in copies[3:]:
+        copy.wait()
+    gain_q = qgain[...]
     runit, rinv = unit_rows(rk[...].astype(f32))
     rnormed = (runit * gain_k).astype(bf16)
     rkn[...] = rnormed
@@ -203,17 +220,16 @@
         here = pl.multiple_of((j - base) * CHUNK, CHUNK)
         values = vals[pl.ds(at, CHUNK), :]
         keys_t = kn_t[j]
-        dkey = jnp.zeros((CHUNK, HD), f32)
-        dvalue = jnp.zeros((CHUNK, HD), f32)
         for c0 in range(0, COLS, CG):
             cols = slice(c0, c0 + CG)
             scale = jnp.exp2(maxima[j, :, cols] - top[:, cols]) * factor[:, cols]
             weights = probs[pl.ds(at, CHUNK), cols] * scale
             dweights = mm(values, gr_t[:, cols])
-            dscores = (weights * (dweights - delta[:, cols])).astype(bf16)
-            dvalue = dvalue + mm(weights.astype(bf16), gr[cols, :])
-            dkey = dkey + mm(dscores, qn[cols, :])
-            dq_t[:, cols] = dq_t[:, cols] + mm(keys_t, dscores)
+            weights_b[:, cols] = weights.astype(bf16)
+            dscores_b[:, cols] = (weights * (dweights - delta[:, cols])).astype(bf16)
+        dvalue = mm(weights_b[...], gr[...])
+        dkey = mm(dscores_b[...], qn[...])
+        dq_t[...] = dq_t[...] + mm(keys_t, dscores_b[...])
         dkey = dkey * SCALING
         out[pl.ds(here, CHUNK), :HD] = dkey
         out[pl.ds(here, CHUNK), HD:] = dvalue
@@ -248,8 +264,6 @@
     key_terms = key_terms + jnp.sum(dkey * runit, axis=0, keepdims=True)
 
     query_terms = jnp.zeros((1, HD), f32)
-    copies[2].wait()
-    copies[3].wait()
     for part, out in enumerate((pdq, rdq)):
         q = held.at[part]
         for pair in range(GROUPS // 2):
@@ -265,11 +279,10 @@
     terms[:, HD:] = jnp.broadcast_to(key_terms, (EXTRA, HD))
 
 
-def attention(info, raw, arrays):
+def attention(info, arrays):
     f32, bf16 = jnp.float32, jnp.bfloat16
     vmem = pl.BlockSpec(memory_space=pltpu.VMEM)
     smem = pl.BlockSpec(memory_space=pltpu.SMEM)
-    anywhere = pl.BlockSpec(memory_space=pl.ANY)
     out_shape = (
         jax.ShapeDtypeStruct((HALF + EXTRA, 2 * HD), f32),
         jax.ShapeDtypeStruct((HALF + EXTRA, 2 * HD), f32),
@@ -297,20 +310,31 @@
         pltpu.VMEM((2, ROWS, GROUPS * HD), bf16),
         pltpu.VMEM((ROWS, HD), bf16),
         pltpu.VMEM((ROWS, HD), bf16),
-        pltpu.SemaphoreType.DMA((4,)),
+        pltpu.VMEM((CHUNK, COLS), bf16),
+        pltpu.VMEM((CHUNK, COLS), bf16),
+        pltpu.VMEM((COLS, HD), bf16),
+        pltpu.VMEM((HD, COLS), bf16),
+        pltpu.VMEM((COLS, HD), bf16),
+        pltpu.VMEM((HD, COLS), bf16),
+        pltpu.VMEM((1, COLS), f32),
+        pltpu.VMEM((1, HD), f32),
+        pltpu.VMEM((1, HD), f32),
+        pltpu.VMEM((HALF, 2 * HD), bf16),
+        pltpu.VMEM((HALF, 2 * HD), bf16),
+        pltpu.SemaphoreType.DMA((len(arrays),)),
     ]
     return pl.pallas_call(
         attention_kernel,
         out_shape=out_shape,
-        in_specs=[smem] + [anywhere] * len(raw) + [vmem] * len(arrays),
+        in_specs=[smem] + [pl.BlockSpec(memory_space=pl.ANY)] * len(arrays),
         out_specs=tuple([vmem] * len(out_shape)),
         scratch_shapes=scratch,
-        compiler_params=pltpu.CompilerParams(vmem_limit_bytes=48 * 1024 * 1024),
+        compiler_params=pltpu.CompilerParams(vmem_limit_bytes=56 * 1024 * 1024),
         cost_estimate=pl.CostEstimate(
             flops=10 * KEYS * COLS * HD, bytes_accessed=8 << 20, transcendentals=KEYS * COLS
         ),
         interpret=INTERPRET,
-    )(info, *raw, *arrays)
+    )(info, *arrays)
 
 
 def exchange(array, axis):
@@ -353,18 +377,20 @@
     return total, terms
 
 
-def first_stage_kernel(keep, got, terms, message):
+def first_stage_kernel(keep, got, message):
     rows = NZ * ROWS
     largest = keep[HALF : HALF + 1, :] + got[HALF : HALF + 1, :]
 
     def blocks(i):
         return keep[i * rows : (i + 1) * rows, :] + got[i * rows : (i + 1) * rows, :]
 
-    pack_message(message, rows, NX, blocks, largest, terms[0:1, :])
-
-
-def second_stage_kernel(got, message):
-    total, terms = unpack_message(got, NZ * ROWS, NX)
+    pack_message(message, rows, NX, blocks, largest, jnp.zeros((1, 2 * HD), jnp.float32))
+
+
+def second_stage_kernel(got, all_terms, message):
+    total, _ = unpack_message(got, NZ * ROWS, NX)
+    row = lax.broadcasted_iota(jnp.int32, all_terms.shape, 0) & (EXTRA - 1)
+    terms = jnp.sum(jnp.where(row == 0, all_terms[...], 0.0), axis=0, keepdims=True)
     largest = jnp.max(jnp.abs(total), axis=0, keepdims=True)
     pack_message(message, ROWS, NZ, lambda i: total[i * ROWS : (i + 1) * ROWS], largest, terms)
 
@@ -390,16 +416,6 @@
         cost_estimate=pl.CostEstimate(flops=1 << 20, bytes_accessed=4 << 20, transcendentals=0),
         interpret=INTERPRET,
     )(*arrays)
-
-
-def sum_over_heads(terms):
-    heads = lax.axis_size("head")
-    step = 1
-    while step < heads:
-        pairs = [(i, i ^ step) for i in range(heads)]
-        terms = terms + lax.ppermute(terms, "head", pairs)
-        step *= 2
-    return terms + swap_core(terms)
 
 
 def per_device(
@@ -417,34 +433,42 @@
     query_gain,
     key_gain,
 ):
-    line = NX * NZ
     place = [lax.axis_index(name).astype(jnp.int32)[None] for name in ("x", "z", "core")]
     info = jnp.concatenate([lengths, *place])
     qgain, kgain = query_gain.reshape(1, HD), key_gain.reshape(1, HD)
 
     local = jnp.concatenate([prompt_key, prompt_value], axis=1)
-    copies = jnp.broadcast_to(local[None], (line,) + local.shape)
-    own = exchange(copies.reshape(line * ROWS, 2 * HD), ("x", "z"))
+    own = lax.all_gather(lax.all_gather(local, "z", axis=0, tiled=True), "x", axis=0, tiled=True)
     raw = [prompt_query, prompt_grad, prompt_out, response_query[0], response_grad[0], response_out[0]]
     prepared = prepare(raw, qgain)
     own, prepared = lax.optimization_barrier((own, prepared))
     other = swap_core(own)
     keep, give, terms, pdq, rdq, rdk, rdv = attention(
         info,
-        [prompt_query, response_query[0], response_key[0], response_value[0]],
-        [*prepared, own, other, qgain, kgain],
+        [
+            own,
+            other,
+            kgain,
+            response_key[0],
+            response_value[0],
+            *prepared,
+            qgain,
+            prompt_query,
+            response_query[0],
+        ],
     )
 
     got = swap_core(give)
-    terms = sum_over_heads(terms)
+    terms = jnp.sum(lax.all_gather(terms, "head", axis=0), axis=0)
+    terms = lax.all_gather(terms, ("x", "core"), axis=0, tiled=True)
     rows = NZ * ROWS + TAIL
     message = small_kernel(
-        first_stage_kernel, jax.ShapeDtypeStruct((NX, rows, 2 * HD), jnp.float32), keep, got, terms
+        first_stage_kernel, jax.ShapeDtypeStruct((NX, rows, 2 * HD), jnp.float32), keep, got
     )
     message = exchange_halves(message, "x")
     rows = ROWS + TAIL
     message = small_kernel(
-        second_stage_kernel, jax.ShapeDtypeStruct((NZ, rows, 2 * HD), jnp.float32), message
+        second_stage_kernel, jax.ShapeDtypeStruct((NZ, rows, 2 * HD), jnp.float32), message, terms
     )
     message = exchange_halves(message, "z")
     block = jax.ShapeDtypeStruct((ROWS, HD), jnp.bfloat16)

time: 137 us -> 178 us (1.30); the launches traced: 134 us -> 178 us
  blocking collectives: 31.6 us -> 86.9 us
  starting transfers between devices: 43 us -> 9.34 us
  between operations: 1.57 us -> 14.8 us
  waiting for transfers between devices: 27.1 us -> 35.8 us
  local copies, waits for them, and re-layouts: 4.45 us -> 2.62 us
    all_gather x0 -> x3, blocking collectives: none -> 66.9 us  [the longest x1 27.6 us: per_device(): lax.all_gather(local, 'z', axis=0, tiled=True)]
    all_gather x0 -> x1, waiting for transfers between devices: none -> 30.5 us  [per_device(): lax.all_gather(lax.all_gather(local, 'z', axis=0, tiled=True), 'x', axis=...]
    all_to_all x1, waiting for transfers between devices: 21.5 us -> 0.01 us  [exchange(): return lax.all_to_all(array, axis, 0, 0, tiled=True)]
    ppermute x3 -> x0, starting transfers between devices: 14.9 us -> none  [sum_over_heads(): terms = terms + lax.ppermute(terms, 'head', pairs)]
    all_to_all x2 -> x1, blocking collectives: 31.6 us -> 20 us  [exchange(): return lax.all_to_all(array, axis, 0, 0, tiled=True)]
    all_to_all x1, starting transfers between devices: 13.7 us -> 3.52 us  [exchange(): return lax.all_to_all(array, axis, 0, 0, tiled=True)]
    ppermute x3 -> x2, starting transfers between devices: 14.5 us -> 5.78 us  [swap_core(): return lax.ppermute(array, 'core', [(0, 1), (1, 0)])]
    ppermute x3 -> x0, waiting for transfers between devices: 3.27 us -> none  [sum_over_heads(): terms = terms + lax.ppermute(terms, 'head', pairs)]
  transfers between devices with their start and end apart: 7 -> 4, of which waited for: 6 -> 3; matrix products, arithmetic and copies ran while one was open for 0% -> 0% of each run, Pallas kernels for 1% -> 2%
where the time goes in v1:
time: 178 us
  blocking collectives  86.9 us (49%)
  waiting for transfers between devices  35.8 us (20%)
  Pallas kernels  25.9 us (15%)
  between operations  14.8 us (8%)
  starting transfers between devices  9.34 us (5%)
  other arithmetic  2.75 us (2%)
  local copies, waits for them, and re-layouts  2.62 us (1%)
    all_gather x1, waiting for transfers between devices, per_device(): lax.all_gather(lax.all_gather(local, 'z', axis=0, tiled=True), 'x', axis=...  30.5 us
    all_gather x1, blocking collectives, per_device(): lax.all_gather(local, 'z', axis=0, tiled=True)  27.6 us
    pallas_call x1, Pallas kernels, attention(): pl.pallas_call(attention_kernel, out_shape=out_shape, in_specs=[smem] + [...  21.9 us
    all_gather x1, blocking collectives, per_device(): terms = jnp.sum(lax.all_gather(terms, 'head', axis=0), axis=0)  20.4 us
    all_to_all x1, blocking collectives, exchange(): return lax.all_to_all(array, axis, 0, 0, tiled=True)  20 us
    all_gather x1, blocking collectives, per_device(): terms = lax.all_gather(terms, ('x', 'core'), axis=0, tiled=True)  18.9 us
    ppermute x2, starting transfers between devices, swap_core(): return lax.ppermute(array, 'core', [(0, 1), (1, 0)])  5.78 us
    ppermute x2, waiting for transfers between devices, swap_core(): return lax.ppermute(array, 'core', [(0, 1), (1, 0)])  5.25 us
  transfers between devices with their start and end apart: 4, of which 3 were waited for; matrix products, arithmetic and copies ran while one was open for 0% of the time, Pallas kernels for 2%

profile of v1, /device:TPU:1, one launch (start us, length us, event | category | flops | bytes accessed | tf_op | source)
XLA Modules:
  0.0 178.0 jit_solution(10791385208508946468)
XLA Ops:
  7.2 0.0 all-gather.3.cloned.1.call-start
  7.2 0.7 pad_maximum_fusion
  8.0 27.6 %all_gather.15 = bf16[512,256]{1,0:T(8,128)(2,1)} all-gather(bf16[64,256]{1,0:T(8,128)(2,1)S(1)} %pad_maximum_fusion), channel_id=1, replica_groups=mesh['x'=4,'z'=8,'core'=2,'head'=8] {'z'}, dimensions={0}, use_global_device_ids=true | all-gather | bytes 294912 | tf_op jit(solution)/shard_map/all_gather | solution.py:441
  35.6 0.0 all-gather.3.cloned.1.call-update
  35.6 2.7 %shard_map.188 = (bf16[1024,128]{1,0:T(8,128)(2,1)}, bf16[128,1024]{1,0:T(8,128)(2,1)}, bf16[1024,128]{1,0:T(8,128)(2,1)}, bf16[128,1024]{1,0:T(8,128)(2,1)}, f32[1,1024]{1,0:T(1,128)}) custom-call(bf16[64,1024]{1,0:T(8,128)(2,1)} %pq_in.3, bf16[64,1024]{1,0:T(8,128)(2,1)} %pg_in.1, bf16[64,1024]{1,0:T(8,128)(2,1)} %po_in.1, bf16[64,1024]{1,0:T(8,128)(2,1)} %bitcast.21, ...), custom_call_target="tpu_custom_call" | custom-call | flops 5242880 | bytes 2097152 | tf_op jit(solution)/shard_map/pallas_call | solution.py:92
  38.3 30.5 %all-gather.3.cloned.1.call-done.own_in = bf16[2048,256]{1,0:T(8,128)(2,1)} async-done(((bf16[512,256]{1,0:T(8,128)(2,1)}), bf16[2048,256]{1,0:T(8,128)(2,1)}) %all-gather.3.cloned.1.call-update) | async-done | bytes 1048592 | tf_op jit(solution)/shard_map/all_gather | solution.py:441
  68.8 3.5 %collective-permute-start = (bf16[2048,256]{1,0:T(8,128)(2,1)}, bf16[2048,256]{1,0:T(8,128)(2,1)S(1)}, u32[]{:S(2)}, u32[]{:S(2)}) collective-permute-start(bf16[2048,256]{1,0:T(8,128)(2,1)} %all-gather.3.cloned.1.call-done.own_in), channel_id=1, source_target_pairs={{0,8},{8,0},{1,9},{9,1},{2,10},{10,2},{3,11},{11,3},{4,12},{12,4},... | collective-permute-start | bytes 3145736 | tf_op jit(solution)/shard_map/ppermute | solution.py:350
  72.9 0.6 pad_add_fusion.info
  73.5 1.3 collective-permute-done.other_in
  74.7 0.0 copy-start.4
  74.8 1.0 copy-done.4
  75.8 21.9 %shard_map.189 = (f32[2056,256]{1,0:T(8,128)}, f32[2056,256]{1,0:T(8,128)}, f32[8,256]{1,0:T(8,128)}, bf16[64,1024]{1,0:T(8,128)(2,1)}, bf16[64,1024]{1,0:T(8,12...) custom-call(s32[4]{0:T(128)} %pad_add_fusion.info, bf16[2048,256]{1,0:T(8,128)(2,1)} %all-gather.3.cloned.1.call-done.own_in, ...), custom_call_target="tpu_custom_call" | custom-call | flops 5368709120 | bytes 8388608 | tf_op jit(solution)/shard_map/pallas_call | solution.py:326
  97.7 2.3 %collective-permute-start.1 = (f32[2056,256]{1,0:T(8,128)}, f32[2056,256]{1,0:T(8,128)S(1)}, u32[]{:S(2)}, u32[]{:S(2)}) collective-permute-start(f32[2056,256]{1,0:T(8,128)} %get-tuple-element.43), channel_id=1, source_target_pairs={{0,8},{8,0},{1,9},{9,1},{2,10},{10,2},{3,11},{11,3},{4,12},{12,4},... | collective-permute-start | bytes 6316040 | tf_op jit(solution)/shard_map/ppermute | solution.py:350
  100.0 4.0 %collective-permute-done.1.got = f32[2056,256]{1,0:T(8,128)S(1)} collective-permute-done((f32[2056,256]{1,0:T(8,128)}, f32[2056,256]{1,0:T(8,128)S(1)}, u32[]{:S(2)}, u32[]{:S(2)}) %collective-permute-start.1) | collective-permute-done | bytes 2105376 | tf_op jit(solution)/shard_map/ppermute | solution.py:350
  104.0 0.0 copy-start
  104.0 1.6 copy-done
  105.6 0.2 shard_map.190
  105.8 0.0 copy-start.3
  105.8 1.2 convert_element_type.14
  107.0 3.5 %all-to-all-start = ((f16[4,528,256]{2,1,0:T(8,128)(2,1)}), f16[4,528,256]{2,1,0:T(8,128)(2,1)S(1)}, u32[]{:S(2)}, u32[]{:S(2)}) async-start(f16[4,528,256]{2,1,0:T(8,128)(2,1)} %convert_element_type.14), calls=%async_computation | async-start | bytes 2162688 | tf_op jit(solution)/shard_map/all_to_all | solution.py:341
  110.5 0.0 copy-done.3
  110.5 20.4 %all-gather = f32[64,256]{1,0:T(8,128)S(1)} all-gather(f32[8,256]{1,0:T(8,128)S(1)} %copy-done.3), channel_id=2, replica_groups=mesh['x'=4,'z'=8,'core'=2,'head'=8] {'head'}, dimensions={0}, use_global_device_ids=true | all-gather | bytes 73728 | tf_op jit(solution)/shard_map/all_gather | solution.py:462
  130.9 18.9 %all_gather.19.all_terms = f32[64,256]{1,0:T(8,128)S(1)} all-gather(f32[8,256]{1,0:T(8,128)S(1)} %bitcast_reduce_fusion), channel_id=1, replica_groups=mesh['x'=4,'z'=8,'core'=2,'head'=8] {'x','core'}, dimensions={0}, use_global_device_ids=true | all-gather | bytes 73728 | tf_op jit(solution)/shard_map/all_gather | solution.py:463
  149.8 0.0 all-to-all-done
  149.9 0.2 convert_element_type.15.got
  150.0 0.0 copy-start.1
  150.0 0.0 copy-start.2
  150.1 0.2 shard_map.191
  150.3 0.1 convert_element_type.16
  150.3 20.0 %all_to_all.12 = f16[8,80,256]{2,1,0:T(8,128)(2,1)S(1)} all-to-all(f16[8,80,256]{2,1,0:T(8,128)(2,1)S(1)} %convert_element_type.16), channel_id=1, replica_groups=mesh['x'=4,'z'=8,'core'=2,'head'=8] {'z'}, dimensions={0} | all-to-all | bytes 655360 | tf_op jit(solution)/shard_map/all_to_all | solution.py:341
  170.3 0.1 convert_element_type.17.got
  170.4 0.0 copy-done.1
  170.4 0.0 copy-done.2
  170.4 0.8 shard_map.192
  (1 shorter events, 0.0 us)
Async XLA Ops:
  7.2 61.6 %all-gather.3.cloned.1.call-start = ((), (), s32[]{:S(2)}) async-start(), calls=%async_computation.2 | async-start | bytes 1310720 | tf_op jit(solution)/shard_map/all_gather | solution.py:441
  68.8 6.0 %collective-permute-start = (bf16[2048,256]{1,0:T(8,128)(2,1)}, bf16[2048,256]{1,0:T(8,128)(2,1)S(1)}, u32[]{:S(2)}, u32[]{:S(2)}) collective-permute-start(bf16[2048,256]{1,0:T(8,128)(2,1)} %all-gather.3.cloned.1.call-done.own_in), channel_id=1, source_target_pairs={{0,8},{8,0},{1,9},{9,1},{2,10},{10,2},{3,11},{11,3},{4,12},{12,4},... | collective-permute-start | bytes 3145736 | tf_op jit(solution)/shard_map/ppermute | solution.py:350
  74.7 1.0 copy-start.4
  97.7 6.3 %collective-permute-start.1 = (f32[2056,256]{1,0:T(8,128)}, f32[2056,256]{1,0:T(8,128)S(1)}, u32[]{:S(2)}, u32[]{:S(2)}) collective-permute-start(f32[2056,256]{1,0:T(8,128)} %get-tuple-element.43), channel_id=1, source_target_pairs={{0,8},{8,0},{1,9},{9,1},{2,10},{10,2},{3,11},{11,3},{4,12},{12,4},... | collective-permute-start | bytes 6316040 | tf_op jit(solution)/shard_map/ppermute | solution.py:350
  104.0 1.6 copy-start
  105.8 4.7 %copy-start.3 = (f32[8,256]{1,0:T(8,128)S(1)}, f32[8,256]{1,0:T(8,128)}, u32[]{:S(2)}) copy-start(f32[8,256]{1,0:T(8,128)} %get-tuple-element.44) | copy-start | bytes 24580
  107.0 42.9 %all-to-all-start = ((f16[4,528,256]{2,1,0:T(8,128)(2,1)}), f16[4,528,256]{2,1,0:T(8,128)(2,1)S(1)}, u32[]{:S(2)}, u32[]{:S(2)}) async-start(f16[4,528,256]{2,1,0:T(8,128)(2,1)} %convert_element_type.14), calls=%async_computation | async-start | bytes 2162688 | tf_op jit(solution)/shard_map/all_to_all | solution.py:341
  150.0 20.3 %copy-start.1 = (bf16[64,128]{1,0:T(8,128)(2,1)S(1)}, bf16[64,128]{1,0:T(8,128)(2,1)}, u32[]{:S(2)}) copy-start(bf16[64,128]{1,0:T(8,128)(2,1)} %keys.1) | copy-start | bytes 49156
  150.0 20.3 %copy-start.2 = (f32[128]{0:T(128)S(1)}, f32[128]{0:T(128)}, u32[]{:S(2)}) copy-start(f32[128]{0:T(128)} %param.25) | copy-start | bytes 1540
Sparse Core Ops, SparseCore 0:
  35.7 33.0 all-gather.2

commit v2 on v1

--- a/solution.py
+++ b/solution.py
@@ -99,7 +99,7 @@
             pltpu.VMEM((1, HD), f32),
             pltpu.SemaphoreType.DMA((len(arrays) + 1,)),
         ],
-        compiler_params=pltpu.CompilerParams(vmem_limit_bytes=56 * 1024 * 1024),
+        compiler_params=pltpu.CompilerParams(vmem_limit_bytes=8 * 1024 * 1024),
         cost_estimate=pl.CostEstimate(flops=COLS * HD * 40, bytes_accessed=2 << 20, transcendentals=0),
         interpret=INTERPRET,
     )(*arrays, qgain)
@@ -107,7 +107,7 @@
 
 def attention_kernel(
     info, own_in, other_in, kgain_in, rk_in, rv_in, qn_in, qn_t_in, gr_in, gr_t_in, delta_in, qgain_in,
-    pq_in, rq_in, keep, send, terms, pdq, rdq, rdk, rdv,
+    pq_in, rq_in, keep, send, pdq, rdq, rdk, rdv,
     kn, kn_t, vals, kunit, rkn, rkn_t, probs, rprobs, maxima, top, total, factor, dq_t, held, rk, rv,
     weights_b, dscores_b, qn, qn_t, gr, gr_t, delta, qgain, kgain, kv_own, kv_other, sems,
 ):
@@ -275,8 +275,9 @@
             out[:, 2 * pair * HD : (2 * pair + 1) * HD] = raw[:ROWS]
             out[:, (2 * pair + 1) * HD : (2 * pair + 2) * HD] = raw[ROWS:]
 
-    terms[:, :HD] = jnp.broadcast_to(query_terms, (EXTRA, HD))
-    terms[:, HD:] = jnp.broadcast_to(key_terms, (EXTRA, HD))
+    for out in (keep, send):
+        out[HALF + 1 : HALF + 2, :HD] = query_terms
+        out[HALF + 1 : HALF + 2, HD:] = key_terms
 
 
 def attention(info, arrays):
@@ -286,7 +287,6 @@
     out_shape = (
         jax.ShapeDtypeStruct((HALF + EXTRA, 2 * HD), f32),
         jax.ShapeDtypeStruct((HALF + EXTRA, 2 * HD), f32),
-        jax.ShapeDtypeStruct((EXTRA, 2 * HD), f32),
         jax.ShapeDtypeStruct((ROWS, GROUPS * HD), bf16),
         jax.ShapeDtypeStruct((ROWS, GROUPS * HD), bf16),
         jax.ShapeDtypeStruct((ROWS, HD), bf16),
@@ -329,7 +329,7 @@
         in_specs=[smem] + [pl.BlockSpec(memory_space=pl.ANY)] * len(arrays),
         out_specs=tuple([vmem] * len(out_shape)),
         scratch_shapes=scratch,
-        compiler_params=pltpu.CompilerParams(vmem_limit_bytes=56 * 1024 * 1024),
+        compiler_params=pltpu.CompilerParams(vmem_limit_bytes=48 * 1024 * 1024),
         cost_estimate=pl.CostEstimate(
             flops=10 * KEYS * COLS * HD, bytes_accessed=8 << 20, transcendentals=KEYS * COLS
         ),
@@ -341,9 +341,15 @@
     return lax.all_to_all(array, axis, 0, 0, tiled=True)
 
 
-def exchange_halves(message, axis):
-    halves = message.astype(jnp.float16).reshape(-1, 2 * HD)
-    return exchange(halves, axis).astype(jnp.float32).reshape(message.shape)
+def exchange_copies(array, axis):
+    count = lax.axis_size(axis)
+    copies = jnp.broadcast_to(array[None], (count,) + array.shape)
+    return exchange(copies.reshape((-1,) + array.shape[1:]), axis)
+
+
+def exchange_halves(halves, axis):
+    got = exchange(halves.reshape(-1, 2 * HD), axis)
+    return got.astype(jnp.float32).reshape(halves.shape)
 
 
 def swap_core(array):
@@ -377,13 +383,16 @@
     return total, terms
 
 
-def first_stage_kernel(keep, got, message):
+def first_stage_kernel(keep, got, message, terms):
     rows = NZ * ROWS
     largest = keep[HALF : HALF + 1, :] + got[HALF : HALF + 1, :]
 
     def blocks(i):
         return keep[i * rows : (i + 1) * rows, :] + got[i * rows : (i + 1) * rows, :]
 
+    terms[...] = jnp.broadcast_to(
+        keep[HALF + 1 : HALF + 2, :] + got[HALF + 1 : HALF + 2, :], terms.shape
+    )
     pack_message(message, rows, NX, blocks, largest, jnp.zeros((1, 2 * HD), jnp.float32))
 
 
@@ -438,12 +447,12 @@
     qgain, kgain = query_gain.reshape(1, HD), key_gain.reshape(1, HD)
 
     local = jnp.concatenate([prompt_key, prompt_value], axis=1)
-    own = lax.all_gather(lax.all_gather(local, "z", axis=0, tiled=True), "x", axis=0, tiled=True)
+    own = exchange_copies(local, ("x", "z"))
     raw = [prompt_query, prompt_grad, prompt_out, response_query[0], response_grad[0], response_out[0]]
     prepared = prepare(raw, qgain)
     own, prepared = lax.optimization_barrier((own, prepared))
     other = swap_core(own)
-    keep, give, terms, pdq, rdq, rdk, rdv = attention(
+    keep, give, pdq, rdq, rdk, rdv = attention(
         info,
         [
             own,
@@ -459,18 +468,25 @@
     )
 
     got = swap_core(give)
-    terms = jnp.sum(lax.all_gather(terms, "head", axis=0), axis=0)
-    terms = lax.all_gather(terms, ("x", "core"), axis=0, tiled=True)
     rows = NZ * ROWS + TAIL
-    message = small_kernel(
-        first_stage_kernel, jax.ShapeDtypeStruct((NX, rows, 2 * HD), jnp.float32), keep, got
-    )
-    message = exchange_halves(message, "x")
+    message, terms = small_kernel(
+        first_stage_kernel,
+        (
+            jax.ShapeDtypeStruct((NX, rows, 2 * HD), jnp.float32),
+            jax.ShapeDtypeStruct((EXTRA, 2 * HD), jnp.float32),
+        ),
+        keep,
+        got,
+    )
+    halves, terms = lax.optimization_barrier((message.astype(jnp.float16), terms))
+    message = exchange_halves(halves, "x")
+    terms = exchange_copies(terms, "head").reshape(-1, EXTRA, 2 * HD).sum(axis=0)
+    terms = exchange_copies(terms, "x")
     rows = ROWS + TAIL
     message = small_kernel(
         second_stage_kernel, jax.ShapeDtypeStruct((NZ, rows, 2 * HD), jnp.float32), message, terms
     )
-    message = exchange_halves(message, "z")
+    message = exchange_halves(message.astype(jnp.float16), "z")
     block = jax.ShapeDtypeStruct((ROWS, HD), jnp.bfloat16)
     gain = jax.ShapeDtypeStruct((1, HD), jnp.float32)
     pdk, pdv, query_total, key_total = small_kernel(

time: 178 us -> 138 us (0.78)
  the two profiles are of different devices: /device:TPU:1 before, /device:TPU:2 now
where the time goes in v2:
time: 138 us; the launch traced here: 137 us
  waiting for transfers between devices  46 us (33%)
  blocking collectives  29.9 us (22%)
  starting transfers between devices  28.4 us (21%)
  Pallas kernels  23.7 us (17%)
  local copies, waits for them, and re-layouts  5.06 us (4%)
  other arithmetic  2.44 us (2%)
  between operations  1.54 us (1%)
    all_to_all x3, waiting for transfers between devices, exchange(): return lax.all_to_all(array, axis, 0, 0, tiled=True)  39.9 us
    all_to_all x2, blocking collectives, exchange(): return lax.all_to_all(array, axis, 0, 0, tiled=True)  29.9 us
    all_to_all x3, starting transfers between devices, exchange(): return lax.all_to_all(array, axis, 0, 0, tiled=True)  24.5 us
    pallas_call x1, Pallas kernels, attention(): pl.pallas_call(attention_kernel, out_shape=out_shape, in_specs=[smem] + [...  20.8 us
    ppermute x2, waiting for transfers between devices, swap_core(): return lax.ppermute(array, 'core', [(0, 1), (1, 0)])  6.11 us
    ppermute x2, starting transfers between devices, swap_core(): return lax.ppermute(array, 'core', [(0, 1), (1, 0)])  3.96 us
    unnamed x30, local copies, waits for them, and re-layouts  3.32 us
  transfers between devices with their start and end apart: 5, of which 5 were waited for; matrix products, arithmetic and copies ran while one was open for 0% of the time, Pallas kernels for 1%

profile of v2, /device:TPU:2, one launch (start us, length us, event | category | flops | bytes accessed | tf_op | source)
XLA Modules:
  0.0 137.1 jit_solution(13371142074331180375)
XLA Ops:
  0.6 0.0 copy-start.4
  0.6 0.0 copy-start.8
  0.7 0.0 copy-start.2
  0.7 0.0 copy-start.3
  0.7 0.0 copy-start.5
  0.7 0.0 copy-start
  0.7 0.0 copy-start.1
  0.7 0.0 copy-start.7
  0.7 0.0 copy-start.14
  0.7 0.0 copy-start.13
  0.7 0.9 pad_maximum_fusion
  1.6 1.1 broadcast_in_dim.39
  2.7 13.5 %all-to-all-start = ((bf16[32,64,256]{2,1,0:T(8,128)(2,1)}), bf16[32,64,256]{2,1,0:T(8,128)(2,1)S(1)}, u32[]{:S(2)}, u32[]{:S(2)}) async-start(bf16[32,64,256]{2,1,0:T(8,128)(2,1)} %broadcast_in_dim.39), calls=%async_computation | async-start | bytes 2097152 | tf_op jit(solution)/shard_map/all_to_all | solution.py:341
  16.2 0.0 copy-done.4
  16.2 0.0 copy-done.8
  16.2 0.0 copy-done.2
  16.2 0.0 copy-done.3
  16.2 0.0 copy-done.5
  16.3 0.0 copy-done
  16.3 0.0 copy-done.1
  16.3 1.7 %shard_map.188 = (bf16[1024,128]{1,0:T(8,128)(2,1)S(1)}, bf16[128,1024]{1,0:T(8,128)(2,1)S(1)}, bf16[1024,128]{1,0:T(8,128)(2,1)S(1)}, bf16[128,1024]{1,0:T(8,128)(2,1)S(1)}, f32[1,1024]{1,0:T(1,128)S(1)}) custom-call(bf16[64,1024]{1,0:T(8,128)(2,1)S(1)} %copy-done.4, bf16[64,1024]{1,0:T(8,128)(2,1)S(1)} %copy-done, bf16[64,1024]{1,0:T(8,128)(2,1)S(1)} %copy-done.1, ...), custom_call_target="tpu_custom_call" | custom-call | flops 5242880 | bytes 2097152 | tf_op jit(solution)/shard_map/pallas_call | solution.py:92
  17.9 0.0 copy-start.9
  18.0 0.7 copy-done.9
  18.7 0.0 copy-start.11
  18.7 0.7 copy-done.11
  19.3 22.9 %all-to-all-done = bf16[32,64,256]{2,1,0:T(8,128)(2,1)S(1)} async-done(((bf16[32,64,256]{2,1,0:T(8,128)(2,1)}), bf16[32,64,256]{2,1,0:T(8,128)(2,1)S(1)}, u32[]{:S(2)}, u32[]{:S(2)}) %all-to-all-start) | async-done | bytes 1048608 | tf_op jit(solution)/shard_map/all_to_all | solution.py:341
  42.3 1.9 %collective-permute-start = (bf16[2048,256]{1,0:T(8,128)(2,1)S(1)}, bf16[2048,256]{1,0:T(8,128)(2,1)S(1)}, u32[]{:S(2)}, u32[]{:S(2)}) collective-permute-start(bf16[2048,256]{1,0:T(8,128)(2,1)S(1)} %bitcast.17), channel_id=1, source_target_pairs={{0,8},{8,0},{1,9},{9,1},{2,10},{10,2},{3,11},{11,3},{4,12},{12,4},... | collective-permute-start | bytes 3145736 | tf_op jit(solution)/shard_map/ppermute | solution.py:356
  44.9 0.1 pad_add_fusion.info
  44.9 1.9 %collective-permute-done.other_in = bf16[2048,256]{1,0:T(8,128)(2,1)S(1)} collective-permute-done((bf16[2048,256]{1,0:T(8,128)(2,1)S(1)}, bf16[2048,256]{1,0:T(8,128)(2,1)S(1)}, u32[]{:S(2)}, u32[]{:S(2)}) %collective-permute-start) | collective-permute-done | bytes 1048608 | tf_op jit(solution)/shard_map/ppermute | solution.py:356
  46.8 0.0 copy-done.7
  46.8 0.0 copy-done.14
  46.8 0.0 copy-done.13
  46.8 0.0 copy-start.10
  46.9 0.9 copy-done.10
  47.8 0.0 copy-start.12
  47.8 0.9 copy-done.12
  48.7 20.8 %shard_map.189 = (f32[2056,256]{1,0:T(8,128)S(1)}, f32[2056,256]{1,0:T(8,128)}, bf16[64,1024]{1,0:T(8,128)(2,1)}, bf16[64,1024]{1,0:T(8,128)(2,1)}, bf16[64,128]{1,0:T(8,128)(2,1)}, /*index=5*/bf16[64,128]{1,0:T(8,128)(2,1)}) custom-call(s32[4]{0:T(128)S(1)} %pad_add_fusion.info, bf16[2048,256]{1,0:T(8,128)(2,1)S(1)} %bitcast.18, ...), custom_call_target="tpu_custom_call" | custom-call | flops 5368709120 | bytes 8388608 | tf_op jit(solution)/shard_map/pallas_call | solution.py:326
  69.6 2.1 %collective-permute-start.1 = (f32[2056,256]{1,0:T(8,128)}, f32[2056,256]{1,0:T(8,128)S(1)}, u32[]{:S(2)}, u32[]{:S(2)}) collective-permute-start(f32[2056,256]{1,0:T(8,128)} %get-tuple-element.46), channel_id=1, source_target_pairs={{0,8},{8,0},{1,9},{9,1},{2,10},{10,2},{3,11},{11,3},{4,12},{12,4},... | collective-permute-start | bytes 6316040 | tf_op jit(solution)/shard_map/ppermute | solution.py:356
  71.6 4.2 %collective-permute-done.1.got = f32[2056,256]{1,0:T(8,128)S(1)} collective-permute-done((f32[2056,256]{1,0:T(8,128)}, f32[2056,256]{1,0:T(8,128)S(1)}, u32[]{:S(2)}, u32[]{:S(2)}) %collective-permute-start.1) | collective-permute-done | bytes 2105376 | tf_op jit(solution)/shard_map/ppermute | solution.py:356
  75.8 0.2 shard_map.190
  76.1 1.2 convert_element_type.14
  77.3 15.3 %all_to_all.35 = f32[8,8,256]{2,1,0:T(8,128)S(1)} all-to-all(f32[8,8,256]{2,1,0:T(8,128)S(1)} %broadcast_in_dim.40), channel_id=1, replica_groups=mesh['x'=4,'z'=8,'core'=2,'head'=8] {'head'}, dimensions={0} | all-to-all | bytes 131072 | tf_op jit(solution)/shard_map/all_to_all | solution.py:341
  92.5 6.3 %all-to-all-start.1 = ((f16[4,528,256]{2,1,0:T(8,128)(2,1)}), f16[4,528,256]{2,1,0:T(8,128)(2,1)S(1)}, u32[]{:S(2)}, u32[]{:S(2)}) async-start(f16[4,528,256]{2,1,0:T(8,128)(2,1)} %convert_element_type.14), calls=%async_computation.1 | async-start | bytes 2162688 | tf_op jit(solution)/shard_map/all_to_all | solution.py:341
  98.9 13.1 %all-to-all-done.1 = f16[4,528,256]{2,1,0:T(8,128)(2,1)S(1)} async-done(((f16[4,528,256]{2,1,0:T(8,128)(2,1)}), f16[4,528,256]{2,1,0:T(8,128)(2,1)S(1)}, u32[]{:S(2)}, u32[]{:S(2)}) %all-to-all-start.1) | async-done | bytes 1081376 | tf_op jit(solution)/shard_map/all_to_all | solution.py:341
  112.0 0.6 broadcast_in_dim.41
  112.6 4.7 %all-to-all-start.3 = ((f32[4,8,256]{2,1,0:T(8,128)}), f32[4,8,256]{2,1,0:T(8,128)S(1)}, u32[]{:S(2)}, u32[]{:S(2)}) async-start(f32[4,8,256]{2,1,0:T(8,128)} %broadcast_in_dim.41), calls=%async_computation.3 | async-start | bytes 65536 | tf_op jit(solution)/shard_map/all_to_all | solution.py:341
  117.3 0.2 convert_element_type.15.got
  117.5 3.8 %all-to-all-done.3 = f32[4,8,256]{2,1,0:T(8,128)S(1)} async-done(((f32[4,8,256]{2,1,0:T(8,128)}), f32[4,8,256]{2,1,0:T(8,128)S(1)}, u32[]{:S(2)}, u32[]{:S(2)}) %all-to-all-start.3) | async-done | bytes 32800 | tf_op jit(solution)/shard_map/all_to_all | solution.py:341
  121.3 0.0 copy-start.6
  121.3 0.2 shard_map.191
  121.5 0.1 convert_element_type.16
  121.6 14.7 %all_to_all.36 = f16[8,80,256]{2,1,0:T(8,128)(2,1)S(1)} all-to-all(f16[8,80,256]{2,1,0:T(8,128)(2,1)S(1)} %convert_element_type.16), channel_id=1, replica_groups=mesh['x'=4,'z'=8,'core'=2,'head'=8] {'z'}, dimensions={0} | all-to-all | bytes 655360 | tf_op jit(solution)/shard_map/all_to_all | solution.py:341
  136.3 0.1 convert_element_type.17.got
  136.3 0.0 copy-done.6
  136.3 0.8 shard_map.192
  (2 shorter events, 0.0 us)
Async XLA Ops:
  0.6 15.6 %copy-start.4 = (bf16[64,1024]{1,0:T(8,128)(2,1)S(1)}, bf16[64,1024]{1,0:T(8,128)(2,1)}, u32[]{:S(2)}) copy-start(bf16[64,1024]{1,0:T(8,128)(2,1)} %pq_in.3) | copy-start | bytes 393220
  0.6 15.6 %copy-start.8 = (f32[128]{0:T(128)S(1)}, f32[128]{0:T(128)}, u32[]{:S(2)}) copy-start(f32[128]{0:T(128)} %param.24) | copy-start | bytes 1540
  0.7 15.6 %copy-start.2 = (bf16[1,64,1024]{2,1,0:T(8,128)(2,1)S(1)}, bf16[1,64,1024]{2,1,0:T(8,128)(2,1)}, u32[]{:S(2)}) copy-start(bf16[1,64,1024]{2,1,0:T(8,128)(2,1)} %param.22) | copy-start | bytes 393220
  0.7 15.6 %copy-start.3 = (bf16[1,64,1024]{2,1,0:T(8,128)(2,1)S(1)}, bf16[1,64,1024]{2,1,0:T(8,128)(2,1)}, u32[]{:S(2)}) copy-start(bf16[1,64,1024]{2,1,0:T(8,128)(2,1)} %param.21) | copy-start | bytes 393220
  0.7 15.6 %copy-start.5 = (bf16[1,64,1024]{2,1,0:T(8,128)(2,1)S(1)}, bf16[1,64,1024]{2,1,0:T(8,128)(2,1)}, u32[]{:S(2)}) copy-start(bf16[1,64,1024]{2,1,0:T(8,128)(2,1)} %param.18) | copy-start | bytes 393220
  0.7 15.6 %copy-start = (bf16[64,1024]{1,0:T(8,128)(2,1)S(1)}, bf16[64,1024]{1,0:T(8,128)(2,1)}, u32[]{:S(2)}) copy-start(bf16[64,1024]{1,0:T(8,128)(2,1)} %pg_in.1) | copy-start | bytes 393220
  0.7 15.6 %copy-start.1 = (bf16[64,1024]{1,0:T(8,128)(2,1)S(1)}, bf16[64,1024]{1,0:T(8,128)(2,1)}, u32[]{:S(2)}) copy-start(bf16[64,1024]{1,0:T(8,128)(2,1)} %po_in.1) | copy-start | bytes 393220
  0.7 46.1 %copy-start.7 = (f32[128]{0:T(128)S(1)}, f32[128]{0:T(128)}, u32[]{:S(2)}) copy-start(f32[128]{0:T(128)} %param.25) | copy-start | bytes 1540
  0.7 46.1 %copy-start.14 = (bf16[1,64,128]{2,1,0:T(8,128)(2,1)S(1)}, bf16[1,64,128]{2,1,0:T(8,128)(2,1)}, u32[]{:S(2)}) copy-start(bf16[1,64,128]{2,1,0:T(8,128)(2,1)} %param.20) | copy-start | bytes 49156
  0.7 46.1 %copy-start.13 = (bf16[1,64,128]{2,1,0:T(8,128)(2,1)S(1)}, bf16[1,64,128]{2,1,0:T(8,128)(2,1)}, u32[]{:S(2)}) copy-start(bf16[1,64,128]{2,1,0:T(8,128)(2,1)} %param.19) | copy-start | bytes 49156
  2.7 39.6 %all-to-all-start = ((bf16[32,64,256]{2,1,0:T(8,128)(2,1)}), bf16[32,64,256]{2,1,0:T(8,128)(2,1)S(1)}, u32[]{:S(2)}, u32[]{:S(2)}) async-start(bf16[32,64,256]{2,1,0:T(8,128)(2,1)} %broadcast_in_dim.39), calls=%async_computation | async-start | bytes 2097152 | tf_op jit(solution)/shard_map/all_to_all | solution.py:341
  17.9 0.7 copy-start.9
  18.7 0.7 copy-start.11
  42.3 4.5 %collective-permute-start = (bf16[2048,256]{1,0:T(8,128)(2,1)S(1)}, bf16[2048,256]{1,0:T(8,128)(2,1)S(1)}, u32[]{:S(2)}, u32[]{:S(2)}) collective-permute-start(bf16[2048,256]{1,0:T(8,128)(2,1)S(1)} %bitcast.17), channel_id=1, source_target_pairs={{0,8},{8,0},{1,9},{9,1},{2,10},{10,2},{3,11},{11,3},{4,12},{12,4},... | collective-permute-start | bytes 3145736 | tf_op jit(solution)/shard_map/ppermute | solution.py:356
  46.8 1.0 copy-start.10
  47.8 0.9 copy-start.12
  69.6 6.3 %collective-permute-start.1 = (f32[2056,256]{1,0:T(8,128)}, f32[2056,256]{1,0:T(8,128)S(1)}, u32[]{:S(2)}, u32[]{:S(2)}) collective-permute-start(f32[2056,256]{1,0:T(8,128)} %get-tuple-element.46), channel_id=1, source_target_pairs={{0,8},{8,0},{1,9},{9,1},{2,10},{10,2},{3,11},{11,3},{4,12},{12,4},... | collective-permute-start | bytes 6316040 | tf_op jit(solution)/shard_map/ppermute | solution.py:356
  92.5 19.5 %all-to-all-start.1 = ((f16[4,528,256]{2,1,0:T(8,128)(2,1)}), f16[4,528,256]{2,1,0:T(8,128)(2,1)S(1)}, u32[]{:S(2)}, u32[]{:S(2)}) async-start(f16[4,528,256]{2,1,0:T(8,128)(2,1)} %convert_element_type.14), calls=%async_computation.1 | async-start | bytes 2162688 | tf_op jit(solution)/shard_map/all_to_all | solution.py:341
  112.6 8.7 %all-to-all-start.3 = ((f32[4,8,256]{2,1,0:T(8,128)}), f32[4,8,256]{2,1,0:T(8,128)S(1)}, u32[]{:S(2)}, u32[]{:S(2)}) async-start(f32[4,8,256]{2,1,0:T(8,128)} %broadcast_in_dim.41), calls=%async_computation.3 | async-start | bytes 65536 | tf_op jit(solution)/shard_map/all_to_all | solution.py:341
  121.3 15.0 %copy-start.6 = (bf16[64,128]{1,0:T(8,128)(2,1)S(1)}, bf16[64,128]{1,0:T(8,128)(2,1)}, u32[]{:S(2)}) copy-start(bf16[64,128]{1,0:T(8,128)(2,1)} %keys.1) | copy-start | bytes 49156

commit v3 on v1

--- a/solution.py
+++ b/solution.py
@@ -99,7 +99,7 @@
             pltpu.VMEM((1, HD), f32),
             pltpu.SemaphoreType.DMA((len(arrays) + 1,)),
         ],
-        compiler_params=pltpu.CompilerParams(vmem_limit_bytes=56 * 1024 * 1024),
+        compiler_params=pltpu.CompilerParams(vmem_limit_bytes=8 * 1024 * 1024),
         cost_estimate=pl.CostEstimate(flops=COLS * HD * 40, bytes_accessed=2 << 20, transcendentals=0),
         interpret=INTERPRET,
     )(*arrays, qgain)
@@ -329,7 +329,7 @@
         in_specs=[smem] + [pl.BlockSpec(memory_space=pl.ANY)] * len(arrays),
         out_specs=tuple([vmem] * len(out_shape)),
         scratch_shapes=scratch,
-        compiler_params=pltpu.CompilerParams(vmem_limit_bytes=56 * 1024 * 1024),
+        compiler_params=pltpu.CompilerParams(vmem_limit_bytes=42 * 1024 * 1024),
         cost_estimate=pl.CostEstimate(
             flops=10 * KEYS * COLS * HD, bytes_accessed=8 << 20, transcendentals=KEYS * COLS
         ),
@@ -341,9 +341,15 @@
     return lax.all_to_all(array, axis, 0, 0, tiled=True)
 
 
-def exchange_halves(message, axis):
-    halves = message.astype(jnp.float16).reshape(-1, 2 * HD)
-    return exchange(halves, axis).astype(jnp.float32).reshape(message.shape)
+def exchange_copies(array, axis):
+    count = lax.axis_size(axis)
+    copies = jnp.broadcast_to(array[None], (count,) + array.shape)
+    return exchange(copies.reshape((-1,) + array.shape[1:]), axis)
+
+
+def exchange_halves(halves, axis):
+    got = exchange(halves.reshape(-1, 2 * HD), axis)
+    return got.astype(jnp.float32).reshape(halves.shape)
 
 
 def swap_core(array):
@@ -377,20 +383,18 @@
     return total, terms
 
 
-def first_stage_kernel(keep, got, message):
+def first_stage_kernel(keep, got, terms, message):
     rows = NZ * ROWS
     largest = keep[HALF : HALF + 1, :] + got[HALF : HALF + 1, :]
 
     def blocks(i):
         return keep[i * rows : (i + 1) * rows, :] + got[i * rows : (i + 1) * rows, :]
 
-    pack_message(message, rows, NX, blocks, largest, jnp.zeros((1, 2 * HD), jnp.float32))
-
-
-def second_stage_kernel(got, all_terms, message):
-    total, _ = unpack_message(got, NZ * ROWS, NX)
-    row = lax.broadcasted_iota(jnp.int32, all_terms.shape, 0) & (EXTRA - 1)
-    terms = jnp.sum(jnp.where(row == 0, all_terms[...], 0.0), axis=0, keepdims=True)
+    pack_message(message, rows, NX, blocks, largest, terms[0:1, :])
+
+
+def second_stage_kernel(got, message):
+    total, terms = unpack_message(got, NZ * ROWS, NX)
     largest = jnp.max(jnp.abs(total), axis=0, keepdims=True)
     pack_message(message, ROWS, NZ, lambda i: total[i * ROWS : (i + 1) * ROWS], largest, terms)
 
@@ -438,7 +442,7 @@
     qgain, kgain = query_gain.reshape(1, HD), key_gain.reshape(1, HD)
 
     local = jnp.concatenate([prompt_key, prompt_value], axis=1)
-    own = lax.all_gather(lax.all_gather(local, "z", axis=0, tiled=True), "x", axis=0, tiled=True)
+    own = exchange_copies(local, ("x", "z"))
     raw = [prompt_query, prompt_grad, prompt_out, response_query[0], response_grad[0], response_out[0]]
     prepared = prepare(raw, qgain)
     own, prepared = lax.optimization_barrier((own, prepared))
@@ -459,18 +463,17 @@
     )
 
     got = swap_core(give)
-    terms = jnp.sum(lax.all_gather(terms, "head", axis=0), axis=0)
-    terms = lax.all_gather(terms, ("x", "core"), axis=0, tiled=True)
+    terms = exchange_copies(terms, ("core", "head")).reshape(-1, EXTRA, 2 * HD).sum(axis=0)
     rows = NZ * ROWS + TAIL
     message = small_kernel(
-        first_stage_kernel, jax.ShapeDtypeStruct((NX, rows, 2 * HD), jnp.float32), keep, got
-    )
-    message = exchange_halves(message, "x")
+        first_stage_kernel, jax.ShapeDtypeStruct((NX, rows, 2 * HD), jnp.float32), keep, got, terms
+    )
+    message = exchange_halves(message.astype(jnp.float16), "x")
     rows = ROWS + TAIL
     message = small_kernel(
-        second_stage_kernel, jax.ShapeDtypeStruct((NZ, rows, 2 * HD), jnp.float32), message, terms
-    )
-    message = exchange_halves(message, "z")
+        second_stage_kernel, jax.ShapeDtypeStruct((NZ, rows, 2 * HD), jnp.float32), message
+    )
+    message = exchange_halves(message.astype(jnp.float16), "z")
     block = jax.ShapeDtypeStruct((ROWS, HD), jnp.bfloat16)
     gain = jax.ShapeDtypeStruct((1, HD), jnp.float32)
     pdk, pdv, query_total, key_total = small_kernel(

time: 178 us -> 130 us (0.73)
  the two profiles are of different devices: /device:TPU:1 before, /device:TPU:8 now
where the time goes in v3:
time: 130 us
  blocking collectives  48.4 us (37%)
  waiting for transfers between devices  26 us (20%)
  Pallas kernels  25.3 us (19%)
  starting transfers between devices  17.1 us (13%)
  local copies, waits for them, and re-layouts  9.99 us (8%)
  between operations  1.56 us (1%)
  other arithmetic  1.46 us (1%)
    all_to_all x3, blocking collectives, exchange(): return lax.all_to_all(array, axis, 0, 0, tiled=True)  48.4 us
    all_to_all x1, waiting for transfers between devices, exchange(): return lax.all_to_all(array, axis, 0, 0, tiled=True)  24.1 us
    pallas_call x1, Pallas kernels, attention(): pl.pallas_call(attention_kernel, out_shape=out_shape, in_specs=[smem] + [...  20.9 us
    all_to_all x1, starting transfers between devices, exchange(): return lax.all_to_all(array, axis, 0, 0, tiled=True)  13.2 us
    unnamed x42, local copies, waits for them, and re-layouts  8.85 us
    ppermute x2, starting transfers between devices, swap_core(): return lax.ppermute(array, 'core', [(0, 1), (1, 0)])  3.92 us
    pallas_call x3, Pallas kernels, small_kernel(): pl.pallas_call(body, out_shape=out_shape, in_specs=[vmem] * len(arrays),...  2.8 us
  transfers between devices with their start and end apart: 3, of which 2 were waited for; matrix products, arithmetic and copies ran while one was open for 0% of the time, Pallas kernels for 1%

profile of v3, /device:TPU:8, one launch (start us, length us, event | category | flops | bytes accessed | tf_op | source)
XLA Modules:
  0.0 129.9 jit_solution(11487103088633587796)
XLA Ops:
  0.6 0.0 copy-start.4
  0.6 0.0 copy-start.8
  0.7 0.0 copy-start.2
  0.7 0.0 copy-start.3
  0.7 0.0 copy-start.5
  0.7 0.0 copy-start
  0.7 0.0 copy-start.1
  0.7 0.0 copy-start.7
  0.7 0.0 copy-start.20
  0.7 0.0 copy-start.19
  0.7 0.9 pad_maximum_fusion
  1.6 1.1 broadcast_in_dim.33
  2.7 13.2 %all-to-all-start = ((bf16[32,64,256]{2,1,0:T(8,128)(2,1)}), bf16[32,64,256]{2,1,0:T(8,128)(2,1)S(1)}, u32[]{:S(2)}, u32[]{:S(2)}) async-start(bf16[32,64,256]{2,1,0:T(8,128)(2,1)} %broadcast_in_dim.33), calls=%async_computation | async-start | bytes 2097152 | tf_op jit(solution)/shard_map/all_to_all | solution.py:341
  15.9 0.0 copy-done.4
  15.9 0.0 copy-done.8
  15.9 0.0 copy-done.2
  15.9 0.0 copy-done.3
  16.0 0.0 copy-done.5
  16.0 0.0 copy-done
  16.0 0.0 copy-done.1
  16.0 1.7 %shard_map.188 = (bf16[1024,128]{1,0:T(8,128)(2,1)S(1)}, bf16[128,1024]{1,0:T(8,128)(2,1)S(1)}, bf16[1024,128]{1,0:T(8,128)(2,1)S(1)}, bf16[128,1024]{1,0:T(8,128)(2,1)S(1)}, f32[1,1024]{1,0:T(1,128)S(1)}) custom-call(bf16[64,1024]{1,0:T(8,128)(2,1)S(1)} %copy-done.4, bf16[64,1024]{1,0:T(8,128)(2,1)S(1)} %copy-done, bf16[64,1024]{1,0:T(8,128)(2,1)S(1)} %copy-done.1, ...), custom_call_target="tpu_custom_call" | custom-call | flops 5242880 | bytes 2097152 | tf_op jit(solution)/shard_map/pallas_call | solution.py:92
  17.7 0.0 copy-start.11
  17.7 0.7 copy-done.11
  18.4 0.0 copy-start.13
  18.4 0.7 copy-done.13
  19.0 0.0 copy-start.15
  19.0 0.7 copy-done.15
  19.8 0.0 copy-start.17
  19.8 0.7 copy-done.17
  20.4 24.1 %all-to-all-done = bf16[32,64,256]{2,1,0:T(8,128)(2,1)S(1)} async-done(((bf16[32,64,256]{2,1,0:T(8,128)(2,1)}), bf16[32,64,256]{2,1,0:T(8,128)(2,1)S(1)}, u32[]{:S(2)}, u32[]{:S(2)}) %all-to-all-start) | async-done | bytes 1048608 | tf_op jit(solution)/shard_map/all_to_all | solution.py:341
  44.6 1.9 %collective-permute-start = (bf16[2048,256]{1,0:T(8,128)(2,1)S(1)}, bf16[2048,256]{1,0:T(8,128)(2,1)S(1)}, u32[]{:S(2)}, u32[]{:S(2)}) collective-permute-start(bf16[2048,256]{1,0:T(8,128)(2,1)S(1)} %bitcast.16), channel_id=1, source_target_pairs={{0,8},{8,0},{1,9},{9,1},{2,10},{10,2},{3,11},{11,3},{4,12},{12,4},... | collective-permute-start | bytes 3145736 | tf_op jit(solution)/shard_map/ppermute | solution.py:356
  47.1 0.1 pad_add_fusion.info
  47.2 1.9 %collective-permute-done.other_in = bf16[2048,256]{1,0:T(8,128)(2,1)S(1)} collective-permute-done((bf16[2048,256]{1,0:T(8,128)(2,1)S(1)}, bf16[2048,256]{1,0:T(8,128)(2,1)S(1)}, u32[]{:S(2)}, u32[]{:S(2)}) %collective-permute-start) | collective-permute-done | bytes 1048608 | tf_op jit(solution)/shard_map/ppermute | solution.py:356
  49.1 0.0 copy-start.9
  49.1 1.0 copy-done.9
  50.1 0.0 copy-done.7
  50.1 0.0 copy-done.20
  50.1 0.0 copy-done.19
  50.1 0.0 copy-start.10
  50.1 1.2 copy-done.10
  51.3 0.0 copy-start.12
  51.3 0.9 copy-done.12
  52.3 0.0 copy-start.14
  52.3 0.9 copy-done.14
  53.2 0.0 copy-start.16
  53.2 0.9 copy-done.16
  54.2 0.0 copy-start.18
  54.2 0.9 copy-done.18
  55.1 20.9 %shard_map.189 = (f32[2056,256]{1,0:T(8,128)S(1)}, f32[2056,256]{1,0:T(8,128)}, f32[8,256]{1,0:T(8,128)S(1)}, bf16[64,1024]{1,0:T(8,128)(2,1)}, bf16[64,1024]{1,...) custom-call(s32[4]{0:T(128)S(1)} %pad_add_fusion.info, bf16[2048,256]{1,0:T(8,128)(2,1)S(1)} %bitcast.17, ...), custom_call_target="tpu_custom_call" | custom-call | flops 5368709120 | bytes 8388608 | tf_op jit(solution)/shard_map/pallas_call | solution.py:326
  76.0 2.0 %collective-permute-start.1 = (f32[2056,256]{1,0:T(8,128)}, f32[2056,256]{1,0:T(8,128)}, u32[]{:S(2)}, u32[]{:S(2)}) collective-permute-start(f32[2056,256]{1,0:T(8,128)} %get-tuple-element.43), channel_id=1, source_target_pairs={{0,8},{8,0},{1,9},{9,1},{2,10},{10,2},{3,11},{11,3},{4,12},{12,4},... | collective-permute-start | bytes 6316040 | tf_op jit(solution)/shard_map/ppermute | solution.py:356
  78.0 15.6 %all_to_all.27 = f32[16,8,256]{2,1,0:T(8,128)S(1)} all-to-all(f32[16,8,256]{2,1,0:T(8,128)S(1)} %broadcast_in_dim.34), channel_id=1, replica_groups=mesh['x'=4,'z'=8,'core'=2,'head'=8] {'core','head'}, dimensions={0} | all-to-all | bytes 262144 | tf_op jit(solution)/shard_map/all_to_all | solution.py:341
  93.7 0.0 collective-permute-done.1.got
  93.7 1.8 %shard_map.190 = f32[4,528,256]{2,1,0:T(8,128)S(1)} custom-call(f32[2056,256]{1,0:T(8,128)S(1)} %get-tuple-element.42.keep, f32[2056,256]{1,0:T(8,128)} %collective-permute-done.1.got, f32[8,256]{1,0:T(8,128)S(1)} %reduce_sum.9.terms), custom_call_target="tpu_custom_call" | custom-call | flops 1048576 | bytes 4194304 | tf_op jit(solution)/shard_map/pallas_call | solution.py:414
  95.5 0.2 convert_element_type.14
  95.7 17.6 %all_to_all.28 = f16[4,528,256]{2,1,0:T(8,128)(2,1)S(1)} all-to-all(f16[4,528,256]{2,1,0:T(8,128)(2,1)S(1)} %convert_element_type.14), channel_id=1, replica_groups=mesh['x'=4,'z'=8,'core'=2,'head'=8] {'x'}, dimensions={0} | all-to-all | bytes 2162688 | tf_op jit(solution)/shard_map/all_to_all | solution.py:341
  113.4 0.2 convert_element_type.15.got
  113.6 0.0 copy-start.6
  113.6 0.2 shard_map.191
  113.8 0.1 convert_element_type.16
  113.8 15.2 %all_to_all.29 = f16[8,80,256]{2,1,0:T(8,128)(2,1)S(1)} all-to-all(f16[8,80,256]{2,1,0:T(8,128)(2,1)S(1)} %convert_element_type.16), channel_id=1, replica_groups=mesh['x'=4,'z'=8,'core'=2,'head'=8] {'z'}, dimensions={0} | all-to-all | bytes 655360 | tf_op jit(solution)/shard_map/all_to_all | solution.py:341
  129.0 0.1 convert_element_type.17.got
  129.1 0.0 copy-done.6
  129.1 0.8 shard_map.192
  (2 shorter events, 0.0 us)
Async XLA Ops:
  0.6 15.3 %copy-start.4 = (bf16[64,1024]{1,0:T(8,128)(2,1)S(1)}, bf16[64,1024]{1,0:T(8,128)(2,1)}, u32[]{:S(2)}) copy-start(bf16[64,1024]{1,0:T(8,128)(2,1)} %pq_in.3) | copy-start | bytes 393220
  0.6 15.3 %copy-start.8 = (f32[128]{0:T(128)S(1)}, f32[128]{0:T(128)}, u32[]{:S(2)}) copy-start(f32[128]{0:T(128)} %param.24) | copy-start | bytes 1540
  0.7 15.3 %copy-start.2 = (bf16[1,64,1024]{2,1,0:T(8,128)(2,1)S(1)}, bf16[1,64,1024]{2,1,0:T(8,128)(2,1)}, u32[]{:S(2)}) copy-start(bf16[1,64,1024]{2,1,0:T(8,128)(2,1)} %param.22) | copy-start | bytes 393220
  0.7 15.3 %copy-start.3 = (bf16[1,64,1024]{2,1,0:T(8,128)(2,1)S(1)}, bf16[1,64,1024]{2,1,0:T(8,128)(2,1)}, u32[]{:S(2)}) copy-start(bf16[1,64,1024]{2,1,0:T(8,128)(2,1)} %param.21) | copy-start | bytes 393220
  0.7 15.3 %copy-start.5 = (bf16[1,64,1024]{2,1,0:T(8,128)(2,1)S(1)}, bf16[1,64,1024]{2,1,0:T(8,128)(2,1)}, u32[]{:S(2)}) copy-start(bf16[1,64,1024]{2,1,0:T(8,128)(2,1)} %param.18) | copy-start | bytes 393220
  0.7 15.3 %copy-start = (bf16[64,1024]{1,0:T(8,128)(2,1)S(1)}, bf16[64,1024]{1,0:T(8,128)(2,1)}, u32[]{:S(2)}) copy-start(bf16[64,1024]{1,0:T(8,128)(2,1)} %pg_in.1) | copy-start | bytes 393220
  0.7 15.3 %copy-start.1 = (bf16[64,1024]{1,0:T(8,128)(2,1)S(1)}, bf16[64,1024]{1,0:T(8,128)(2,1)}, u32[]{:S(2)}) copy-start(bf16[64,1024]{1,0:T(8,128)(2,1)} %po_in.1) | copy-start | bytes 393220
  0.7 49.4 %copy-start.7 = (f32[128]{0:T(128)S(1)}, f32[128]{0:T(128)}, u32[]{:S(2)}) copy-start(f32[128]{0:T(128)} %param.25) | copy-start | bytes 1540
  0.7 49.4 %copy-start.20 = (bf16[1,64,128]{2,1,0:T(8,128)(2,1)S(1)}, bf16[1,64,128]{2,1,0:T(8,128)(2,1)}, u32[]{:S(2)}) copy-start(bf16[1,64,128]{2,1,0:T(8,128)(2,1)} %param.20) | copy-start | bytes 49156
  0.7 49.4 %copy-start.19 = (bf16[1,64,128]{2,1,0:T(8,128)(2,1)S(1)}, bf16[1,64,128]{2,1,0:T(8,128)(2,1)}, u32[]{:S(2)}) copy-start(bf16[1,64,128]{2,1,0:T(8,128)(2,1)} %param.19) | copy-start | bytes 49156
  2.7 41.8 %all-to-all-start = ((bf16[32,64,256]{2,1,0:T(8,128)(2,1)}), bf16[32,64,256]{2,1,0:T(8,128)(2,1)S(1)}, u32[]{:S(2)}, u32[]{:S(2)}) async-start(bf16[32,64,256]{2,1,0:T(8,128)(2,1)} %broadcast_in_dim.33), calls=%async_computation | async-start | bytes 2097152 | tf_op jit(solution)/shard_map/all_to_all | solution.py:341
  17.7 0.7 copy-start.11
  18.4 0.7 copy-start.13
  19.0 0.7 copy-start.15
  19.8 0.7 copy-start.17
  44.6 4.5 %collective-permute-start = (bf16[2048,256]{1,0:T(8,128)(2,1)S(1)}, bf16[2048,256]{1,0:T(8,128)(2,1)S(1)}, u32[]{:S(2)}, u32[]{:S(2)}) collective-permute-start(bf16[2048,256]{1,0:T(8,128)(2,1)S(1)} %bitcast.16), channel_id=1, source_target_pairs={{0,8},{8,0},{1,9},{9,1},{2,10},{10,2},{3,11},{11,3},{4,12},{12,4},... | collective-permute-start | bytes 3145736 | tf_op jit(solution)/shard_map/ppermute | solution.py:356
  49.1 1.0 copy-start.9
  50.1 1.2 copy-start.10
  51.3 0.9 copy-start.12
  52.3 0.9 copy-start.14
  53.2 0.9 copy-start.16
  54.2 0.9 copy-start.18
  76.0 17.7 %collective-permute-start.1 = (f32[2056,256]{1,0:T(8,128)}, f32[2056,256]{1,0:T(8,128)}, u32[]{:S(2)}, u32[]{:S(2)}) collective-permute-start(f32[2056,256]{1,0:T(8,128)} %get-tuple-element.43), channel_id=1, source_target_pairs={{0,8},{8,0},{1,9},{9,1},{2,10},{10,2},{3,11},{11,3},{4,12},{12,4},... | collective-permute-start | bytes 6316040 | tf_op jit(solution)/shard_map/ppermute | solution.py:356
  113.6 15.5 %copy-start.6 = (bf16[64,128]{1,0:T(8,128)(2,1)S(1)}, bf16[64,128]{1,0:T(8,128)(2,1)}, u32[]{:S(2)}) copy-start(bf16[64,128]{1,0:T(8,128)(2,1)} %keys.1) | copy-start | bytes 49156
